TPU v7x, 256 devices: a whole 4x4x8 slice. The times are simulated.
256 devices in a mesh: grp: 8 (over z), seq: 32 (over y, x, core).
Axes of the slice: x: 4, y: 4, z: 8, core: 2. Of those that a mesh axis runs over, the one named last changes fastest.
Arguments:
- queries: bfloat16 [8, 4096, 640], P('grp', 'seq'), may hold values from -140 to 140
- resp_kv: bfloat16 [8, 4096, 256], P('grp', 'seq'), may hold values from -6 to 6
- grad_out: bfloat16 [8, 4096, 640], P('grp', 'seq'), may hold values from -6 to 6
- prompt_kv: bfloat16 [8, 5, 2048, 256], P('grp', None, 'seq'), may hold values from -5 to 5
- resp_inputs: bfloat16 [8, 4096, 5120], P('grp', 'seq'), may hold values from -6 to 6
- prompt_inputs: bfloat16 [8, 5, 2048, 5120], P('grp', None, 'seq'), may hold values from -6 to 6
- prompt_blocks: int32 [8, 8], P('grp'), may hold values from 1 to 32, 136 in all within a row
- response_order: int32 [8, 64], P('grp'), may hold values from 0 to 63, each once within a row
- response_len: int32 [8, 64], P('grp', 'seq'), may hold values from 1 to 64, 2457 in all within a row
Outputs:
- d_queries: bfloat16 [8, 4096, 640], P('grp', 'seq')
- d_resp_kv: bfloat16 [8, 4096, 256], P('grp', 'seq')
- d_prompt_kv: bfloat16 [8, 5, 2048, 256], P('grp', None, 'seq')
- d_value_weight: bfloat16 [5120, 128], replicated
Inputs may be any that keep to these rules, and one draw needn't show every extreme that they name: `prompt_blocks`: the prompts of a group fill 136 of its 160 block slots; one prompt of each group has 32 blocks. `response_order`: each group's row is a permutation. `response_len`: each group's lengths sum to 2457; one response of each group has 64.
All inputs are finite; a program needn't handle non-finite values.
Results may differ from a plain program's by a relative error of at most 0.019.
Values may be sent and summed in bfloat16 or wider, within the bound.
No kernel may reach another device: no remote copies, remote signals or barrier semaphores. Data moves between devices by JAX's collectives and lax.ppermute only.
A program may use at most 128 MiB of HBM per device.

v0:
```python
import jax
import jax.numpy as jnp
from jax import lax
from jax.sharding import PartitionSpec as P

HD = 128
HEADS = 5
RLEN = 64
RESP_DEV = 2
RPP = 8
PB = 64


def response_grads(query_rows, key_values, live_grad, allowed):
    scaling = HD ** (-0.5)
    query_heads = query_rows.reshape(query_rows.shape[0], HEADS, HD)
    grad_heads = live_grad.reshape(live_grad.shape[0], HEADS, HD)
    key_rows = key_values[:, :HD]
    value_rows = key_values[:, HD:]
    scores = (
        jnp.einsum("qhd,kd->hqk", query_heads, key_rows, preferred_element_type=jnp.float32)
        * scaling
    )
    scores = jnp.where(allowed[None], scores, -1e30)
    row_max = jnp.max(scores, axis=-1, keepdims=True)
    raised = jnp.exp(scores - row_max)
    prob_rows = raised / jnp.sum(raised, axis=-1, keepdims=True)
    prob_half = prob_rows.astype(jnp.bfloat16)
    prob_grad = jnp.einsum(
        "qhd,kd->hqk", grad_heads, value_rows, preferred_element_type=jnp.float32
    )
    row_total = jnp.sum(prob_rows * prob_grad, axis=-1, keepdims=True)
    score_grad = (prob_rows * (prob_grad - row_total)).astype(jnp.bfloat16)
    query_grad = (
        jnp.einsum("hqk,kd->qhd", score_grad, key_rows, preferred_element_type=jnp.float32)
        * scaling
    )
    key_grad = (
        jnp.einsum("hqk,qhd->kd", score_grad, query_heads, preferred_element_type=jnp.float32)
        * scaling
    )
    value_grad = jnp.einsum(
        "hqk,qhd->kd", prob_half, grad_heads, preferred_element_type=jnp.float32
    )
    query_grad = query_grad.reshape(query_rows.shape[0], HEADS * HD).astype(jnp.bfloat16)
    return (query_grad, jnp.concatenate([key_grad, value_grad], axis=1))


def local(
    queries,
    resp_kv,
    grad_out,
    prompt_kv,
    resp_inputs,
    prompt_inputs,
    prompt_blocks,
    response_order,
    response_len,
):
    seq_count = lax.axis_size("seq")
    position = lax.axis_index("seq")
    slot_rows = prompt_kv.shape[1]
    local_kv = prompt_kv[0]
    blocks = prompt_blocks[0]
    arrival = response_order[0]
    prompt_ids = jnp.arange(blocks.shape[0], dtype=jnp.int32)
    picked = (arrival // RPP)[:, None] == prompt_ids[None, :]
    starts = jnp.cumsum(blocks) - blocks
    begin_slot = jnp.sum(jnp.where(picked, starts[None, :], 0), axis=1)
    block_count = jnp.sum(jnp.where(picked, blocks[None, :], 0), axis=1)
    owners = jnp.arange(seq_count, dtype=jnp.int32)
    offset = (owners[None, :] - begin_slot[:, None]) % seq_count
    usable = offset < block_count[:, None]
    located = jnp.minimum((begin_slot[:, None] + offset) // seq_count, slot_rows - 1)
    mine_use = lax.dynamic_slice_in_dim(usable, position * RESP_DEV, RESP_DEV, 0)
    mine_loc = lax.dynamic_slice_in_dim(located, position * RESP_DEV, RESP_DEV, 0)
    everything = lax.all_gather(local_kv, "seq", axis=1, tiled=True)
    everything = everything.reshape(slot_rows * seq_count, PB, 2 * HD)
    fetched = jnp.take(everything, mine_loc * seq_count + owners[None, :], axis=0)
    row_ids = jnp.arange(RLEN, dtype=jnp.int32)
    causal = row_ids[:, None] >= row_ids[None, :]
    live_lengths = response_len[0]
    query_parts = []
    resp_parts = []
    prompt_parts = []
    for member in range(RESP_DEV):
        row_start = member * RLEN
        query_rows = queries[0, row_start : row_start + RLEN]
        kv_rows = resp_kv[0, row_start : row_start + RLEN]
        grad_rows = grad_out[0, row_start : row_start + RLEN]
        prompt_seen = jnp.repeat(mine_use[member], PB)
        allowed = jnp.concatenate(
            [jnp.broadcast_to(prompt_seen[None, :], (RLEN, seq_count * PB)), causal], axis=1
        )
        live_rows = row_ids < live_lengths[member]
        live_grad = jnp.where(live_rows[:, None], grad_rows, jnp.zeros_like(grad_rows))
        key_values = jnp.concatenate(
            [fetched[member].reshape(seq_count * PB, 2 * HD), kv_rows], axis=0
        )
        query_grad, kv_grads = response_grads(query_rows, key_values, live_grad, allowed)
        query_parts.append(query_grad)
        resp_parts.append(kv_grads[seq_count * PB :].astype(jnp.bfloat16))
        prompt_parts.append(kv_grads[: seq_count * PB].reshape(seq_count, PB, 2 * HD))
    partials = jnp.stack(prompt_parts)
    slot_ids = jnp.arange(slot_rows, dtype=jnp.int32)
    one_hot = ((mine_loc[:, :, None] == slot_ids[None, None, :]) & mine_use[:, :, None]).astype(
        jnp.float32
    )
    spread = jnp.einsum(
        "rnl,rnx->lnx",
        one_hot,
        partials.reshape(RESP_DEV, seq_count, PB * 2 * HD),
        precision=lax.Precision.HIGHEST,
    )
    slot_grads = lax.psum_scatter(
        spread.reshape(slot_rows, seq_count * PB, 2 * HD).astype(jnp.bfloat16),
        "seq",
        scatter_dimension=1,
        tiled=True,
    )
    d_queries = jnp.concatenate(query_parts, axis=0)[None]
    d_resp_kv = jnp.concatenate(resp_parts, axis=0)[None]
    d_prompt_kv = slot_grads[None]
    weight_term = jnp.einsum(
        "td,tk->dk", resp_inputs[0], d_resp_kv[0, :, HD:], preferred_element_type=jnp.float32
    )
    weight_term = weight_term + jnp.einsum(
        "std,stk->dk",
        prompt_inputs[0],
        d_prompt_kv[0, :, :, HD:],
        preferred_element_type=jnp.float32,
    )
    summed_grad = lax.psum(weight_term, ("grp", "seq"))
    key_total = lax.axis_size("grp") * seq_count * (RESP_DEV * RLEN + slot_rows * PB)
    d_value_weight = (summed_grad * key_total ** (-0.5)).astype(jnp.bfloat16)
    return (d_queries, d_resp_kv, d_prompt_kv, d_value_weight)


def solution(mesh):
    in_specs = (
        P("grp", "seq", None),
        P("grp", "seq", None),
        P("grp", "seq", None),
        P("grp", None, "seq", None),
        P("grp", "seq", None),
        P("grp", None, "seq", None),
        P("grp", None),
        P("grp", None),
        P("grp", "seq"),
    )
    out_specs = (P("grp", "seq", None), P("grp", "seq", None), P("grp", None, "seq", None), P())
    return jax.shard_map(local, mesh=mesh, in_specs=in_specs, out_specs=out_specs, check_vma=False)
```

profile of v0, /device:TPU:1, one launch (start us, length us, event | category | flops | bytes accessed | tf_op | source)
XLA Modules:
  0.0 517.0 jit_solution(14110752504858313640)
XLA Ops:
  17.3 1.6 fusion.88
  28.4 39.0 %all-gather.3.cloned.1.call-done = bf16[1,5,2048,256]{3,2,1,0:T(8,128)(2,1)} async-done(((bf16[1,5,64,256]{3,2,1,0:T(8,128)(2,1)}), bf16[1,5,2048,256]{3,2,1,0:T(8,128)(2,1)}) %all-gather.3.cloned.1.call-update) | async-done | bytes 5242896 | tf_op jit(solution)/shard_map/all_gather | solution.py:77
  67.4 4.6 gather_fusion
  72.0 1.8 broadcast_select_fusion
  75.3 4.5 fusion.95
  79.8 3.7 convolution_bitcast_fusion.5
  83.5 2.8 multiply_reduce_fusion.1
  86.3 4.4 fusion.90
  90.7 3.7 convolution_bitcast_fusion.3
  94.5 2.7 multiply_reduce_fusion
  101.3 1.5 pad_maximum_fusion.1
  102.8 4.4 stack.10
  107.2 3.0 multiply_convert_fusion
  114.5 4.3 stack.11
  118.8 13.1 %fusion.2 = bf16[5,32,16384]{2,0,1:T(8,128)(2,1)S(1)} fusion(f32[1,32,16384]{2,0,1:T(1,128)} %stack.11, f32[1,32,16384]{2,0,1:T(1,128)} %stack.10, pred[2,32]{0,1:T(8,128)(4,1)S(1)} %copy-done.26, s32[2,32]{0,1:T(8,128)S(1)} %copy.48), kind=kOutput, calls=%fused_computation.4 | convolution fusion | flops 66585216 | bytes 9437504 | tf_op jit(solution)/shard_map/rnl,rnx->lnx/dot_general | solution.py:109
  131.9 5.8 %copy.50 = bf16[5,32,16384]{2,1,0:T(8,128)(2,1)} copy(bf16[5,32,16384]{2,0,1:T(8,128)(2,1)S(1)} %fusion.2) | data formatting | bytes 10485760 | tf_op jit(solution)/shard_map/convert_element_type | solution.py:116
  137.7 8.9 %convert_element_type.57 = bf16[5,2048,256]{2,1,0:T(8,128)(2,1)} reshape(bf16[5,32,16384]{2,1,0:T(8,128)(2,1)} %copy.50) | data formatting | bytes 10485760 | tf_op jit(solution)/shard_map/convert_element_type | solution.py:116
  147.5 88.8 %reduce-scatter.2.cloned.1.call-done = bf16[5,64,256]{2,1,0:T(8,128)(2,1)} async-done(((bf16[5,2048,256]{2,1,0:T(8,128)(2,1)}), bf16[5,64,256]{2,1,0:T(8,128)(2,1)}) %reduce-scatter.2.cloned.1.call-update) | async-done | bytes 163856 | tf_op jit(solution)/shard_map/reduce_scatter | solution.py:115
  236.3 1.9 convolution_bitcast_fusion
  238.2 2.1 fusion.3
  241.0 2.2 fusion.24
  244.5 260.5 %all-reduce.2.cloned.1.call-done = f32[5120,128]{0,1:T(8,128)} async-done(((f32[5120,128]{0,1:T(8,128)}), f32[5120,128]{0,1:T(8,128)}) %all-reduce.2.cloned.1.call-update) | async-done | bytes 2621456 | tf_op jit(solution)/shard_map/psum | solution.py:133
  505.0 3.1 multiply_convert_fusion.2
  508.1 2.4 copy.51
  (117 shorter events, 32.2 us)
Async XLA Ops:
  7.2 229.1 %copy-start = (bf16[1,5,64,5120]{3,2,1,0:T(8,128)(2,1)S(1)}, bf16[1,5,64,5120]{3,2,1,0:T(8,128)(2,1)}, u32[]{:S(2)}) copy-start(bf16[1,5,64,5120]{3,2,1,0:T(8,128)(2,1)} %param.14) | copy-start | bytes 9830404
  7.2 60.2 %all-gather.3.cloned.1.call-start = ((), (), s32[]{:S(2)}) async-start(), calls=%async_computation.3 | async-start | bytes 5406720 | tf_op jit(solution)/shard_map/all_gather | solution.py:77
  7.9 228.4 %reduce-scatter.2.cloned.1.call-start = ((), (), s32[]{:S(2)}) async-start(), calls=%async_computation.1 | async-start | bytes 5406720 | tf_op jit(solution)/shard_map/reduce_scatter | solution.py:115
  67.4 4.6 copy-start.33
  75.3 4.5 copy-start.20
  79.8 3.7 copy-start.8
  79.8 3.7 copy-start.15
  79.8 3.7 copy-start.21
  79.8 3.7 copy-start.24
  79.8 3.7 copy-start.27
  90.7 3.7 copy-start.10
  90.7 3.7 copy-start.13
  90.7 3.7 copy-start.19
  90.7 3.7 copy-start.22
  90.7 3.7 copy-start.29
  94.5 3.6 copy-start.11
  94.5 3.6 copy-start.28
  94.5 3.6 copy-start.31
  102.8 4.4 copy-start.30
  102.8 4.4 copy-start.32
  114.4 4.3 copy-start.26
  146.6 358.4 %all-reduce.2.cloned.1.call-start = ((), (), s32[]{:S(2)}) async-start(), calls=%async_computation.2 | async-start | bytes 5242880 | tf_op jit(solution)/shard_map/psum | solution.py:133
  147.5 90.7 %copy-start.18 = (bf16[1,128,256]{2,1,0:T(8,128)(2,1)}, bf16[1,128,256]{2,1,0:T(8,128)(2,1)S(1)}, u32[]{:S(2)}) copy-start(bf16[1,128,256]{2,1,0:T(8,128)(2,1)S(1)} %maximum_bitcast_fusion.1) | copy-start | bytes 196612
  240.3 2.9 copy-start.23
  (13 other events, 21.6 us)
Sparse Core Ops, SparseCore 0:
  10.6 56.7 all-gather.2
  146.7 89.5 reduce-scatter.1
  242.6 262.3 all-reduce.1
where the time goes:
time: 519 us; the launch traced here: 517 us
  waiting for transfers between devices  389 us (75%)
  local copies, waits for them, and re-layouts  48.7 us (9%)
  matrix products  42.7 us (8%)
  other arithmetic  22.4 us (4%)
  between operations  14.1 us (3%)
    psum x1, waiting for transfers between devices, local(): summed_grad = lax.psum(weight_term, ('grp', 'seq'))  261 us
    reduce_scatter x1, waiting for transfers between devices, local(): lax.psum_scatter(spread.reshape(slot_rows, seq_count * PB, 2 * HD).astype...  88.8 us
    all_gather x1, waiting for transfers between devices, local(): everything = lax.all_gather(local_kv, 'seq', axis=1, tiled=True)  39 us
    convert_element_type x2, local copies, waits for them, and re-layouts, local(): spread.reshape(slot_rows, seq_count * PB, 2 * HD).astype(jnp.bfloat16)  14.7 us
    dot_general x1, matrix products, local(): jnp.einsum('rnl,rnx->lnx', one_hot, partials.reshape(RESP_DEV, seq_count,...  13.1 us
  transfers between devices with their start and end apart: 3, of which 3 were waited for; matrix products, arithmetic and copies ran while one was open for 5% of the time, Pallas kernels for 0%

commit v1 on v0

v1 whole, which is shorter than its diff:
```python
import functools

import jax
import jax.numpy as jnp
from jax import lax
from jax.experimental import pallas as pl
from jax.experimental.pallas import tpu as pltpu
from jax.sharding import PartitionSpec as P

HD = 128
HEADS = 5
RLEN = 64
RESP_DEV = 2
RPP = 8
PB = 64
ROWS = HEADS * RLEN
SCALING = HD ** (-0.5)
LOG2E = 1.4426950408889634
OWN_BLOCKS = 4
NT = (((1,), (1,)), ((), ()))
TN = (((0,), (0,)), ((), ()))


def first_block(blocks_ref, prompt):
    total = jnp.int32(0)
    for i in range(blocks_ref.shape[0]):
        total = total + jnp.where(i < prompt, blocks_ref[i], 0)
    return total


def fill_starts(blocks_ref, starts_ref):
    total = jnp.int32(0)
    for i in range(blocks_ref.shape[0]):
        starts_ref[i] = total
        total = total + blocks_ref[i]


def place_of(response, owner, order_ref, starts_ref, owners, slot_rows):
    begin = starts_ref[order_ref[response] >> 3]
    offset = (owner - begin) & (owners - 1)
    return jnp.minimum((begin + offset) >> (owners.bit_length() - 1), slot_rows - 1)


def pack_kernel(owners, pos_ref, blocks_ref, order_ref, kv_ref, out_ref, starts_ref):
    fill_starts(blocks_ref, starts_ref)
    owner = pos_ref[0]

    def body(response, carry):
        place = place_of(response, owner, order_ref, starts_ref, owners, kv_ref.shape[0])
        out_ref[response] = kv_ref[place]
        return carry

    lax.fori_loop(0, out_ref.shape[0], body, 0)


def attention_kernel(
    owners,
    pos_ref,
    blocks_ref,
    order_ref,
    len_ref,
    query_ref,
    own_ref,
    grad_ref,
    got_ref,
    dq_ref,
    down_ref,
    back_ref,
    score_ref,
    pgrad_ref,
):
    f32, bf16 = jnp.float32, jnp.bfloat16
    chunk = OWN_BLOCKS * PB
    chunks = owners // OWN_BLOCKS
    factor = SCALING * LOG2E
    for member in range(RESP_DEV):
        prompt = order_ref[pos_ref[0] * RESP_DEV + member] >> 3
        begin = first_block(blocks_ref, prompt)
        count = blocks_ref[prompt]
        rows = slice(member * RLEN, (member + 1) * RLEN)
        q = jnp.concatenate(
            [query_ref[rows, h * HD : (h + 1) * HD] for h in range(HEADS)], axis=0
        )
        g = jnp.concatenate([grad_ref[rows, h * HD : (h + 1) * HD] for h in range(HEADS)], axis=0)
        row_ids = lax.broadcasted_iota(jnp.int32, (ROWS, HD), 0) & (RLEN - 1)
        g = jnp.where(row_ids < len_ref[member], g, jnp.zeros_like(g))

        def keys_of(i):
            if i < chunks:
                part = got_ref[i * OWN_BLOCKS : (i + 1) * OWN_BLOCKS, member]
                return part.reshape(chunk, 2 * HD)
            return own_ref[rows, :]

        def rows_of(i):
            return slice(i * chunk, i * chunk + (chunk if i < chunks else RLEN))

        top = jnp.full((8, ROWS), -1e30, f32)
        for i in range(chunks + 1):
            kv = keys_of(i)
            s = lax.dot_general(kv[:, :HD], q, NT, preferred_element_type=f32)
            key_ids = lax.broadcasted_iota(jnp.int32, s.shape, 0)
            if i < chunks:
                offset = ((key_ids >> 6) + (i * OWN_BLOCKS - begin)) & (owners - 1)
                s = jnp.where(offset < count, s, -1e30)
            else:
                query_ids = lax.broadcasted_iota(jnp.int32, s.shape, 1) & (RLEN - 1)
                s = jnp.where(key_ids <= query_ids, s, -1e30)
            score_ref[rows_of(i), :] = s
            top = jnp.maximum(top, jnp.max(s.reshape(-1, 8, ROWS), axis=0))
        top = jnp.max(top, axis=0, keepdims=True)
        total = jnp.zeros((8, ROWS), f32)
        mixed = jnp.zeros((8, ROWS), f32)
        for i in range(chunks + 1):
            kv = keys_of(i)
            pg = lax.dot_general(kv[:, HD:], g, NT, preferred_element_type=f32)
            e = jnp.exp2((score_ref[rows_of(i), :] - top) * factor)
            score_ref[rows_of(i), :] = e
            pgrad_ref[rows_of(i), :] = pg
            total = total + jnp.sum(e.reshape(-1, 8, ROWS), axis=0)
            mixed = mixed + jnp.sum((e * pg).reshape(-1, 8, ROWS), axis=0)
        inverse = 1.0 / jnp.sum(total, axis=0, keepdims=True)
        row_total = jnp.sum(mixed, axis=0, keepdims=True) * inverse
        dqt = jnp.zeros((HD, ROWS), f32)
        for i in range(chunks + 1):
            kv = keys_of(i)
            p = score_ref[rows_of(i), :] * inverse
            ds = (p * (pgrad_ref[rows_of(i), :] - row_total)).astype(bf16)
            dk = lax.dot_general(ds, q, (((1,), (0,)), ((), ())), preferred_element_type=f32)
            dv = lax.dot_general(
                p.astype(bf16), g, (((1,), (0,)), ((), ())), preferred_element_type=f32
            )
            dkv = jnp.concatenate([dk * SCALING, dv], axis=1).astype(bf16)
            if i < chunks:
                back_ref[i * OWN_BLOCKS : (i + 1) * OWN_BLOCKS, member] = dkv.reshape(
                    OWN_BLOCKS, PB, 2 * HD
                )
            else:
                down_ref[rows, :] = dkv
            dqt = dqt + lax.dot_general(kv[:, :HD], ds, TN, preferred_element_type=f32)
        dq = (dqt * SCALING).T.astype(bf16)
        for h in range(HEADS):
            dq_ref[rows, h * HD : (h + 1) * HD] = dq[h * RLEN : (h + 1) * RLEN]


def combine_kernel(owners, pos_ref, blocks_ref, order_ref, got_ref, out_ref, starts_ref, acc_ref):
    fill_starts(blocks_ref, starts_ref)
    owner = pos_ref[0]
    acc_ref[...] = jnp.zeros_like(acc_ref)

    def body(response, carry):
        place = place_of(response, owner, order_ref, starts_ref, owners, out_ref.shape[0])
        acc_ref[place] += got_ref[response].astype(jnp.float32)
        return carry

    lax.fori_loop(0, got_ref.shape[0], body, 0)
    out_ref[...] = acc_ref[...].astype(jnp.bfloat16)


def smem():
    return pl.BlockSpec(memory_space=pltpu.SMEM)


def vmem():
    return pl.BlockSpec(memory_space=pltpu.VMEM)


def params():
    return pltpu.CompilerParams(vmem_limit_bytes=40 * 1024 * 1024)


def grp_sum(part, grp_count):
    own = part.astype(jnp.bfloat16)
    step = 1
    total = part
    while step < grp_count:
        width = min(4, grp_count // step)
        total = own.astype(jnp.float32)
        for k in range(1, width):
            pairs = [(i, i ^ (k * step)) for i in range(grp_count)]
            total = total + lax.ppermute(own, "grp", pairs).astype(jnp.float32)
        own = total.astype(jnp.bfloat16)
        step = step * width
    return total


def local(
    queries,
    resp_kv,
    grad_out,
    prompt_kv,
    resp_inputs,
    prompt_inputs,
    prompt_blocks,
    response_order,
    response_len,
):
    bf16, f32 = jnp.bfloat16, jnp.float32
    owners = lax.axis_size("seq")
    grp_count = lax.axis_size("grp")
    slot_rows = prompt_kv.shape[1]
    responses = owners * RESP_DEV
    pos = lax.axis_index("seq").astype(jnp.int32).reshape(1)
    blocks, order, lengths = prompt_blocks[0], response_order[0], response_len[0]

    packed = pl.pallas_call(
        functools.partial(pack_kernel, owners),
        out_shape=jax.ShapeDtypeStruct((responses, PB, 2 * HD), bf16),
        in_specs=[smem(), smem(), smem(), vmem()],
        out_specs=vmem(),
        scratch_shapes=[pltpu.SMEM((blocks.shape[0],), jnp.int32)],
        compiler_params=params(),
        name="pack",
    )(pos, blocks, order, prompt_kv[0])
    fetched = lax.all_to_all(
        packed.reshape(responses * PB, 2 * HD), "seq", 0, 0, tiled=True
    ).reshape(owners, RESP_DEV, PB, 2 * HD)

    keys = owners * PB + RLEN
    d_queries, d_resp_kv, partials = pl.pallas_call(
        functools.partial(attention_kernel, owners),
        out_shape=(
            jax.ShapeDtypeStruct((RESP_DEV * RLEN, HEADS * HD), bf16),
            jax.ShapeDtypeStruct((RESP_DEV * RLEN, 2 * HD), bf16),
            jax.ShapeDtypeStruct((owners, RESP_DEV, PB, 2 * HD), bf16),
        ),
        in_specs=[smem()] * 4 + [vmem()] * 4,
        out_specs=[vmem()] * 3,
        scratch_shapes=[pltpu.VMEM((keys, ROWS), f32), pltpu.VMEM((keys, ROWS), f32)],
        compiler_params=params(),
        name="attention",
    )(pos, blocks, order, lengths, queries[0], resp_kv[0], grad_out[0], fetched)
    returned = lax.all_to_all(
        partials.reshape(responses * PB, 2 * HD), "seq", 0, 0, tiled=True
    ).reshape(responses, PB, 2 * HD)

    d_prompt = pl.pallas_call(
        functools.partial(combine_kernel, owners),
        out_shape=jax.ShapeDtypeStruct((slot_rows, PB, 2 * HD), bf16),
        in_specs=[smem(), smem(), smem(), vmem()],
        out_specs=vmem(),
        scratch_shapes=[
            pltpu.SMEM((blocks.shape[0],), jnp.int32),
            pltpu.VMEM((slot_rows, PB, 2 * HD), f32),
        ],
        compiler_params=params(),
        name="combine",
    )(pos, blocks, order, returned)

    weight_term = jnp.einsum(
        "td,tk->dk", resp_inputs[0], d_resp_kv[:, HD:], preferred_element_type=f32
    ) + jnp.einsum("std,stk->dk", prompt_inputs[0], d_prompt[:, :, HD:], preferred_element_type=f32)
    width = weight_term.shape[0]
    shares = lax.all_to_all(weight_term.astype(bf16), "seq", 0, 0, tiled=True)
    share = jnp.sum(shares.reshape(owners, width // owners, HD).astype(f32), axis=0)
    key_total = grp_count * owners * (RESP_DEV * RLEN + slot_rows * PB)
    share = (grp_sum(share, grp_count) * key_total ** (-0.5)).astype(bf16)
    copies = jnp.broadcast_to(share[None], (owners,) + share.shape)
    d_value_weight = lax.all_to_all(copies.reshape(width, HD), "seq", 0, 0, tiled=True)
    return (d_queries[None], d_resp_kv[None], d_prompt[None], d_value_weight)


def solution(mesh):
    in_specs = (
        P("grp", "seq", None),
        P("grp", "seq", None),
        P("grp", "seq", None),
        P("grp", None, "seq", None),
        P("grp", "seq", None),
        P("grp", None, "seq", None),
        P("grp", None),
        P("grp", None),
        P("grp", "seq"),
    )
    out_specs = (P("grp", "seq", None), P("grp", "seq", None), P("grp", None, "seq", None), P())
    return jax.shard_map(local, mesh=mesh, in_specs=in_specs, out_specs=out_specs, check_vma=False)
```

time: 519 us -> 159 us (0.31)
  waiting for transfers between devices: 389 us -> 4.83 us
  blocking collectives: 0 us -> 120 us
  local copies, waits for them, and re-layouts: 48.7 us -> 6.08 us
  matrix products: 42.7 us -> 3.45 us
  other arithmetic: 22.4 us -> 1.55 us
  between operations: 14.1 us -> 0.75 us
  Pallas kernels: 0 us -> 11.2 us
  starting transfers between devices: 0.12 us -> 10.7 us
    psum x1 -> x0, waiting for transfers between devices: 261 us -> none  [local(): summed_grad = lax.psum(weight_term, ('grp', 'seq'))]
    all_to_all x0 -> x4, blocking collectives: none -> 120 us  [the longest x1 36.9 us: local(): lax.all_to_all(packed.reshape(responses * PB, 2 * HD), 'seq', 0, 0, tiled...]
    reduce_scatter x1 -> x0, waiting for transfers between devices: 88.8 us -> none  [local(): lax.psum_scatter(spread.reshape(slot_rows, seq_count * PB, 2 * HD).astype...]
    all_gather x1 -> x0, waiting for transfers between devices: 39 us -> none  [local(): everything = lax.all_gather(local_kv, 'seq', axis=1, tiled=True)]
    dot_general x11 -> x2, matrix products: 33.9 us -> 3.45 us  [the longest x1 1.87 us: local(): jnp.einsum('std,stk->dk', prompt_inputs[0], d_prompt[:, :, HD:], preferre...]
    convert_element_type x3 -> x1, local copies, waits for them, and re-layouts: 14.7 us -> 2.44 us  [local(): shares = lax.all_to_all(weight_term.astype(bf16), 'seq', 0, 0, tiled=True)]
    pallas_call x0 -> x3, Pallas kernels: none -> 11.2 us  [the longest x1 7.33 us: local(): pl.pallas_call(functools.partial(attention_kernel, owners), out_shape=(ja...]
    ppermute x0 -> x4, starting transfers between devices: none -> 10.7 us  [grp_sum(): total = total + lax.ppermute(own, 'grp', pairs).astype(jnp.float32)]
  transfers between devices with their start and end apart: 3 -> 4, of which waited for: 3 -> 3; matrix products, arithmetic and copies ran while one was open for 5% -> 0% of each run, Pallas kernels for 0% -> 0%
where the time goes in v1:
time: 159 us; the launch traced here: 158 us
  blocking collectives  120 us (75%)
  Pallas kernels  11.2 us (7%)
  starting transfers between devices  10.7 us (7%)
  local copies, waits for them, and re-layouts  6.08 us (4%)
  waiting for transfers between devices  4.83 us (3%)
  matrix products  3.45 us (2%)
    all_to_all x1, blocking collectives, local(): lax.all_to_all(packed.reshape(responses * PB, 2 * HD), 'seq', 0, 0, tiled...  36.9 us
    all_to_all x1, blocking collectives, local(): lax.all_to_all(partials.reshape(responses * PB, 2 * HD), 'seq', 0, 0, til...  31.9 us
    all_to_all x1, blocking collectives, local(): lax.all_to_all(copies.reshape(width, HD), 'seq', 0, 0, tiled=True)  25.9 us
    all_to_all x1, blocking collectives, local(): shares = lax.all_to_all(weight_term.astype(bf16), 'seq', 0, 0, tiled=True)  25 us
    ppermute x4, starting transfers between devices, grp_sum(): total = total + lax.ppermute(own, 'grp', pairs).astype(jnp.float32)  10.7 us
    pallas_call x1, Pallas kernels, local(): pl.pallas_call(functools.partial(attention_kernel, owners), out_shape=(ja...  7.33 us
    ppermute x4, waiting for transfers between devices, grp_sum(): total = total + lax.ppermute(own, 'grp', pairs).astype(jnp.float32)  4.83 us
    unnamed x21, local copies, waits for them, and re-layouts  3.47 us
  transfers between devices with their start and end apart: 4, of which 3 were waited for; matrix products, arithmetic and copies ran while one was open for 0% of the time, Pallas kernels for 0%

profile of v1, /device:TPU:1, one launch (start us, length us, event | category | flops | bytes accessed | tf_op | source)
XLA Modules:
  0.0 158.3 jit_solution(12892572685489828738)
XLA Ops:
  0.6 0.0 copy-start
  0.7 1.1 copy-done.1
  1.7 0.7 copy-done.5
  2.4 0.7 copy-done.6
  3.0 1.5 pack.1
  4.5 0.0 copy-start.2
  4.5 36.9 %all_to_all.36 = bf16[32,128,256]{2,1,0:T(8,128)(2,1)S(1)} all-to-all(bf16[32,128,256]{2,1,0:T(8,128)(2,1)S(1)} %bitcast.29), channel_id=1, replica_groups=mesh['grp'=8,'seq'=32] {'seq'}, dimensions={0} | all-to-all | bytes 4194304 | tf_op jit(solution)/shard_map/all_to_all | solution.py:214
  41.5 7.3 %attention.1 = (bf16[128,640]{1,0:T(8,128)(2,1)}, bf16[128,256]{1,0:T(8,128)(2,1)}, bf16[32,2,64,256]{3,2,1,0:T(8,128)(2,1)S(1)}) custom-call(s32[1]{0:T(128)} %bitcast.pos_ref, s32[8]{0:T(128)S(1)} %bitcast.36, s32[64]{0:T(128)S(1)} %bitcast.39, s32[2]{0:T(128)S(1)} %bitcast.41, bf16[128,640]{1,0:T(8,128)(2,1)S(1)} %bitcast.32, ...), custom_call_target="tpu_custom_call" | custom-call | tf_op jit(solution)/shard_map/attention/pallas_call | solution.py:219
  48.8 31.9 %all_to_all.37 = bf16[32,128,256]{2,1,0:T(8,128)(2,1)S(1)} all-to-all(bf16[32,128,256]{2,1,0:T(8,128)(2,1)S(1)} %bitcast.30), channel_id=1, replica_groups=mesh['grp'=8,'seq'=32] {'seq'}, dimensions={0} | all-to-all | bytes 4194304 | tf_op jit(solution)/shard_map/all_to_all | solution.py:232
  80.7 2.4 %combine.1 = bf16[5,64,256]{2,1,0:T(8,128)(2,1)} custom-call(s32[1]{0:T(128)} %bitcast.pos_ref, s32[8]{0:T(128)S(1)} %bitcast.37, s32[64]{0:T(128)S(1)} %bitcast.40, bf16[64,64,256]{2,1,0:T(8,128)(2,1)S(1)} %bitcast.28), custom_call_target="tpu_custom_call" | custom-call | tf_op jit(solution)/shard_map/combine/pallas_call | solution.py:236
  83.1 1.9 %convolution_bitcast_fusion = f32[128,5120]{1,0:T(8,128)S(1)} fusion(bf16[1,5,64,5120]{3,2,1,0:T(8,128)(2,1)S(1)} %copy-done, bf16[5,64,256]{2,1,0:T(8,128)(2,1)} %combine.1), kind=kOutput, calls=%fused_computation.1 | convolution fusion | flops 419430400 | bytes 5980160 | tf_op jit(solution)/shard_map/std,stk->dk/dot_general | solution.py:251
  85.0 1.6 %fusion.1 = bf16[5120,128]{0,1:T(8,128)(2,1)} fusion(f32[128,5120]{1,0:T(8,128)S(1)} %convolution_bitcast_fusion, bf16[1,128,5120]{2,1,0:T(8,128)(2,1)S(1)} %copy-done.8, bf16[128,256]{1,0:T(8,128)(2,1)S(1)} %copy-done.9), kind=kOutput, calls=%fused_computation.3 | convolution fusion | flops 169082880 | bytes 5275648 | tf_op jit(solution)/shard_map/td,tk->dk/dot_general | solution.py:249
  86.6 2.4 %copy.13 = bf16[5120,128]{1,0:T(8,128)(2,1)} copy(bf16[5120,128]{0,1:T(8,128)(2,1)} %fusion.1) | data formatting | bytes 2621440 | tf_op jit(solution)/shard_map/convert_element_type | solution.py:253
  89.1 25.0 %all_to_all.38 = bf16[32,160,128]{2,1,0:T(8,128)(2,1)} all-to-all(bf16[32,160,128]{2,1,0:T(8,128)(2,1)} %bitcast.43), channel_id=1, replica_groups=mesh['grp'=8,'seq'=32] {'seq'}, dimensions={0} | all-to-all | bytes 2621440 | tf_op jit(solution)/shard_map/all_to_all | solution.py:253
  114.1 1.5 reduce_sum.12
  115.6 4.4 %collective-permute-start.2 = (bf16[160,128]{1,0:T(8,128)(2,1)S(1)}, bf16[160,128]{1,0:T(8,128)(2,1)S(1)}, u32[]{:S(2)}, u32[]{:S(2)}) collective-permute-start(bf16[160,128]{1,0:T(8,128)(2,1)S(1)} %reduce_sum.12), channel_id=1, source_target_pairs={{0,96},{32,64},{64,32},{96,0},{128,224},{160,192},{192,160},{224,1... | collective-permute-start | bytes 122888 | tf_op jit(solution)/shard_map/ppermute | solution.py:180
  120.0 0.4 collective-permute-start
  120.4 1.5 collective-permute-done.2
  121.8 2.0 %collective-permute-done.1 = bf16[160,128]{1,0:T(8,128)(2,1)S(1)} collective-permute-done((bf16[160,128]{1,0:T(8,128)(2,1)S(1)}, bf16[160,128]{1,0:T(8,128)(2,1)S(1)}, u32[]{:S(2)}, u32[]{:S(2)}) %collective-permute-start.1) | collective-permute-done | bytes 40992 | tf_op jit(solution)/shard_map/ppermute | solution.py:180
  123.9 5.9 %collective-permute-start.3 = (bf16[160,128]{1,0:T(8,128)(2,1)S(1)}, bf16[160,128]{1,0:T(8,128)(2,1)S(1)}, u32[]{:S(2)}, u32[]{:S(2)}) collective-permute-start(bf16[160,128]{1,0:T(8,128)(2,1)S(1)} %add_convert_fusion), channel_id=1, source_target_pairs={{0,128},{32,160},{64,192},{96,224},{128,0},{160,32},{192,64},{224,... | collective-permute-start | bytes 122888 | tf_op jit(solution)/shard_map/ppermute | solution.py:180
  129.7 1.4 collective-permute-done.3
  131.2 0.2 broadcast_in_dim.18
  131.3 25.9 %all_to_all.39 = bf16[32,160,128]{2,1,0:T(8,128)(2,1)S(1)} all-to-all(bf16[32,160,128]{2,1,0:T(8,128)(2,1)S(1)} %broadcast_in_dim.18), channel_id=1, replica_groups=mesh['grp'=8,'seq'=32] {'seq'}, dimensions={0} | all-to-all | bytes 2621440 | tf_op jit(solution)/shard_map/all_to_all | solution.py:258
  157.2 1.1 copy.15
  (19 shorter events, 0.1 us)
Async XLA Ops:
  0.6 82.5 %copy-start = (bf16[1,5,64,5120]{3,2,1,0:T(8,128)(2,1)S(1)}, bf16[1,5,64,5120]{3,2,1,0:T(8,128)(2,1)}, u32[]{:S(2)}) copy-start(bf16[1,5,64,5120]{3,2,1,0:T(8,128)(2,1)} %param.14) | copy-start | bytes 9830404
  0.7 1.1 copy-start.1
  1.7 0.7 copy-start.5
  2.4 0.7 copy-start.6
  4.5 37.0 %copy-start.2 = (bf16[1,128,640]{2,1,0:T(8,128)(2,1)S(1)}, bf16[1,128,640]{2,1,0:T(8,128)(2,1)}, u32[]{:S(2)}) copy-start(bf16[1,128,640]{2,1,0:T(8,128)(2,1)} %param.9) | copy-start | bytes 491524
  4.5 37.0 %copy-start.3 = (bf16[1,128,640]{2,1,0:T(8,128)(2,1)S(1)}, bf16[1,128,640]{2,1,0:T(8,128)(2,1)}, u32[]{:S(2)}) copy-start(bf16[1,128,640]{2,1,0:T(8,128)(2,1)} %param.11) | copy-start | bytes 491524
  4.5 37.0 %copy-start.4 = (bf16[1,128,256]{2,1,0:T(8,128)(2,1)S(1)}, bf16[1,128,256]{2,1,0:T(8,128)(2,1)}, u32[]{:S(2)}) copy-start(bf16[1,128,256]{2,1,0:T(8,128)(2,1)} %param.10) | copy-start | bytes 196612
  4.5 37.0 %copy-start.7 = (s32[1,2]{1,0:T(1,128)S(1)}, s32[1,2]{1,0:T(1,128)}, u32[]{:S(2)}) copy-start(s32[1,2]{1,0:T(1,128)} %param.17) | copy-start | bytes 28
  83.1 1.9 %copy-start.8 = (bf16[1,128,5120]{2,1,0:T(8,128)(2,1)S(1)}, bf16[1,128,5120]{2,1,0:T(8,128)(2,1)}, u32[]{:S(2)}) copy-start(bf16[1,128,5120]{2,1,0:T(8,128)(2,1)} %param.13) | copy-start | bytes 3932164
  83.1 1.9 %copy-start.9 = (bf16[128,256]{1,0:T(8,128)(2,1)S(1)}, bf16[128,256]{1,0:T(8,128)(2,1)}, u32[]{:S(2)}) copy-start(bf16[128,256]{1,0:T(8,128)(2,1)} %get-tuple-element.8) | copy-start | bytes 196612
  115.6 6.3 %collective-permute-start.2 = (bf16[160,128]{1,0:T(8,128)(2,1)S(1)}, bf16[160,128]{1,0:T(8,128)(2,1)S(1)}, u32[]{:S(2)}, u32[]{:S(2)}) collective-permute-start(bf16[160,128]{1,0:T(8,128)(2,1)S(1)} %reduce_sum.12), channel_id=1, source_target_pairs={{0,96},{32,64},{64,32},{96,0},{128,224},{160,192},{192,160},{224,1... | collective-permute-start | bytes 122888 | tf_op jit(solution)/shard_map/ppermute | solution.py:180
  120.0 3.8 %collective-permute-start.1 = (bf16[160,128]{1,0:T(8,128)(2,1)S(1)}, bf16[160,128]{1,0:T(8,128)(2,1)S(1)}, u32[]{:S(2)}, u32[]{:S(2)}) collective-permute-start(bf16[160,128]{1,0:T(8,128)(2,1)S(1)} %reduce_sum.12), channel_id=1, source_target_pairs={{0,64},{32,96},{64,0},{96,32},{128,192},{160,224},{192,128},{224,1... | collective-permute-start | bytes 122888 | tf_op jit(solution)/shard_map/ppermute | solution.py:180
  120.0 3.8 %collective-permute-start = (bf16[160,128]{1,0:T(8,128)(2,1)S(1)}, bf16[160,128]{1,0:T(8,128)(2,1)S(1)}, u32[]{:S(2)}, u32[]{:S(2)}) collective-permute-start(bf16[160,128]{1,0:T(8,128)(2,1)S(1)} %reduce_sum.12), channel_id=1, source_target_pairs={{0,32},{32,0},{64,96},{96,64},{128,160},{160,128},{192,224},{224,1... | collective-permute-start | bytes 122888 | tf_op jit(solution)/shard_map/ppermute | solution.py:180
  123.9 7.3 %collective-permute-start.3 = (bf16[160,128]{1,0:T(8,128)(2,1)S(1)}, bf16[160,128]{1,0:T(8,128)(2,1)S(1)}, u32[]{:S(2)}, u32[]{:S(2)}) collective-permute-start(bf16[160,128]{1,0:T(8,128)(2,1)S(1)} %add_convert_fusion), channel_id=1, source_target_pairs={{0,128},{32,160},{64,192},{96,224},{128,0},{160,32},{192,64},{224,... | collective-permute-start | bytes 122888 | tf_op jit(solution)/shard_map/ppermute | solution.py:180

commit v2 on v1

v2 whole, which is shorter than its diff:
```python
import functools

import jax
import jax.numpy as jnp
from jax import lax
from jax.experimental import pallas as pl
from jax.experimental.pallas import tpu as pltpu
from jax.sharding import PartitionSpec as P

HD = 128
HEADS = 5
RLEN = 64
RESP_DEV = 2
RPP = 8
PB = 64
ROWS = HEADS * RLEN
SCALING = HD ** (-0.5)
LOG2E = 1.4426950408889634
OWN_BLOCKS = 4
CHUNK = 640
NN = (((1,), (0,)), ((), ()))
NT = (((1,), (1,)), ((), ()))
TN = (((0,), (0,)), ((), ()))


def first_block(blocks_ref, prompt):
    total = jnp.int32(0)
    for i in range(blocks_ref.shape[0]):
        total = total + jnp.where(i < prompt, blocks_ref[i], 0)
    return total


def fill_starts(blocks_ref, starts_ref):
    total = jnp.int32(0)
    for i in range(blocks_ref.shape[0]):
        starts_ref[i] = total
        total = total + blocks_ref[i]


def place_of(response, owner, order_ref, starts_ref, owners, slot_rows):
    begin = starts_ref[order_ref[response] >> 3]
    offset = (owner - begin) & (owners - 1)
    return jnp.minimum((begin + offset) >> (owners.bit_length() - 1), slot_rows - 1)


def pack_kernel(
    owners,
    pos_ref,
    blocks_hbm,
    order_hbm,
    kv_hbm,
    out_ref,
    blocks_ref,
    order_ref,
    starts_ref,
    kv_ref,
    sems,
):
    copies = [
        pltpu.make_async_copy(blocks_hbm.at[0], blocks_ref, sems.at[0]),
        pltpu.make_async_copy(order_hbm.at[0], order_ref, sems.at[1]),
        pltpu.make_async_copy(kv_hbm.at[0], kv_ref, sems.at[2]),
    ]
    for copy in copies:
        copy.start()
    for copy in copies:
        copy.wait()
    fill_starts(blocks_ref, starts_ref)
    owner = pos_ref[0]

    def body(response, carry):
        place = place_of(response, owner, order_ref, starts_ref, owners, kv_ref.shape[0])
        out_ref[response] = kv_ref[place]
        return carry

    lax.fori_loop(0, out_ref.shape[0], body, 0, unroll=8)


def stacked_heads(ref, rows):
    return jnp.concatenate([ref[rows, h * HD : (h + 1) * HD] for h in range(HEADS)], axis=0)


def attention_kernel(
    owners,
    pos_ref,
    blocks_ref,
    order_ref,
    len_ref,
    query_ref,
    own_ref,
    grad_ref,
    got_ref,
    down_v_ref,
    back_v_ref,
    sgrad_hbm,
    score_ref,
    pgrad_ref,
    sgrad_ref,
    sems,
):
    f32, bf16 = jnp.float32, jnp.bfloat16
    chunk = OWN_BLOCKS * PB
    chunks = owners // OWN_BLOCKS
    factor = SCALING * LOG2E
    for member in range(RESP_DEV):
        prompt = order_ref[pos_ref[0] * RESP_DEV + member] >> 3
        begin = first_block(blocks_ref, prompt)
        count = blocks_ref[prompt]
        rows = slice(member * RLEN, (member + 1) * RLEN)
        q = stacked_heads(query_ref, rows)
        g = stacked_heads(grad_ref, rows)
        row_ids = lax.broadcasted_iota(jnp.int32, (ROWS, HD), 0) & (RLEN - 1)
        g = jnp.where(row_ids < len_ref[member], g, jnp.zeros_like(g))

        def part_of(i):
            return slice(i * OWN_BLOCKS, (i + 1) * OWN_BLOCKS)

        def rows_of(i):
            return slice(i * chunk, i * chunk + (chunk if i < chunks else RLEN))

        top = jnp.full((8, ROWS), -1e30, f32)
        for i in range(chunks + 1):
            if i < chunks:
                k = got_ref[part_of(i), member, :, :HD].reshape(chunk, HD)
            else:
                k = own_ref[rows, :HD]
            s = lax.dot_general(k, q, NT, preferred_element_type=f32)
            key_ids = lax.broadcasted_iota(jnp.int32, s.shape, 0)
            if i < chunks:
                offset = ((key_ids >> 6) + (i * OWN_BLOCKS - begin)) & (owners - 1)
                s = jnp.where(offset < count, s, -1e30)
            else:
                query_ids = lax.broadcasted_iota(jnp.int32, s.shape, 1) & (RLEN - 1)
                s = jnp.where(key_ids <= query_ids, s, -1e30)
            score_ref[rows_of(i), :] = s
            top = jnp.maximum(top, jnp.max(s.reshape(-1, 8, ROWS), axis=0))
        top = jnp.max(top, axis=0, keepdims=True)
        total = jnp.zeros((8, ROWS), f32)
        mixed = jnp.zeros((8, ROWS), f32)
        for i in range(chunks + 1):
            if i < chunks:
                v = got_ref[part_of(i), member, :, HD:].reshape(chunk, HD)
            else:
                v = own_ref[rows, HD:]
            pg = lax.dot_general(v, g, NT, preferred_element_type=f32)
            e = jnp.exp2((score_ref[rows_of(i), :] - top) * factor)
            score_ref[rows_of(i), :] = e
            pgrad_ref[rows_of(i), :] = pg
            total = total + jnp.sum(e.reshape(-1, 8, ROWS), axis=0)
            mixed = mixed + jnp.sum((e * pg).reshape(-1, 8, ROWS), axis=0)
        inverse = 1.0 / jnp.sum(total, axis=0, keepdims=True)
        row_total = jnp.sum(mixed, axis=0, keepdims=True) * inverse
        for i in range(chunks + 1):
            p = score_ref[rows_of(i), :] * inverse
            sgrad_ref[member, rows_of(i), :] = (
                p * (pgrad_ref[rows_of(i), :] - row_total)
            ).astype(bf16)
            dv = lax.dot_general(p.astype(bf16), g, NN, preferred_element_type=f32).astype(bf16)
            if i < chunks:
                back_v_ref[part_of(i), member] = dv.reshape(OWN_BLOCKS, PB, HD)
            else:
                down_v_ref[rows, :] = dv
        pltpu.make_async_copy(sgrad_ref.at[member], sgrad_hbm.at[member], sems.at[member]).start()
    for member in range(RESP_DEV):
        pltpu.make_async_copy(sgrad_ref.at[member], sgrad_hbm.at[member], sems.at[member]).wait()


def query_key_kernel(
    owners,
    query_ref,
    own_ref,
    got_ref,
    sgrad_hbm,
    down_v_ref,
    dq_ref,
    down_ref,
    back_k_ref,
    sgrad_ref,
    sems,
):
    copies = [
        pltpu.make_async_copy(sgrad_hbm.at[member], sgrad_ref.at[member], sems.at[member])
        for member in range(RESP_DEV)
    ]
    for copy in copies:
        copy.start()
    f32, bf16 = jnp.float32, jnp.bfloat16
    chunk = OWN_BLOCKS * PB
    chunks = owners // OWN_BLOCKS
    for member in range(RESP_DEV):
        rows = slice(member * RLEN, (member + 1) * RLEN)
        q = stacked_heads(query_ref, rows)
        copies[member].wait()
        dqt = jnp.zeros((HD, ROWS), f32)
        for i in range(chunks + 1):
            part = slice(i * OWN_BLOCKS, (i + 1) * OWN_BLOCKS)
            ds = sgrad_ref[member, i * chunk : i * chunk + (chunk if i < chunks else RLEN), :]
            dk = lax.dot_general(ds, q, NN, preferred_element_type=f32) * SCALING
            if i < chunks:
                k = got_ref[part, member, :, :HD].reshape(chunk, HD)
                back_k_ref[part, member] = dk.astype(bf16).reshape(OWN_BLOCKS, PB, HD)
            else:
                k = own_ref[rows, :HD]
                down_ref[rows, :HD] = dk.astype(bf16)
            dqt = dqt + lax.dot_general(k, ds, TN, preferred_element_type=f32)
        dq = (dqt * SCALING).T.astype(bf16)
        for h in range(HEADS):
            dq_ref[rows, h * HD : (h + 1) * HD] = dq[h * RLEN : (h + 1) * RLEN]
    down_ref[:, HD:] = down_v_ref[...]


def half_weights(resp_in_ref, resp_grad_ref, prompt_in_ref, prompt_grad):
    f32 = jnp.float32
    term = lax.dot_general(resp_in_ref[...], resp_grad_ref[...], TN, preferred_element_type=f32)
    more = lax.dot_general(prompt_in_ref[...], prompt_grad, TN, preferred_element_type=f32)
    return (term + more).astype(jnp.bfloat16)


def sum_blocks(owners, pos_ref, blocks_ref, order_ref, got_ref, starts_ref, acc_ref):
    fill_starts(blocks_ref, starts_ref)
    owner = pos_ref[0]
    acc_ref[...] = jnp.zeros_like(acc_ref)

    def body(response, carry):
        place = place_of(response, owner, order_ref, starts_ref, owners, acc_ref.shape[0])
        acc_ref[place] += got_ref[response].astype(jnp.float32)
        return carry

    lax.fori_loop(0, got_ref.shape[0], body, 0, unroll=8)


def combine_kernel(
    owners,
    pos_ref,
    blocks_ref,
    order_ref,
    got_ref,
    resp_in_ref,
    resp_grad_ref,
    prompt_in_ref,
    out_ref,
    weight_ref,
    starts_ref,
    acc_ref,
):
    @pl.when(pl.program_id(0) == 0)
    def _():
        sum_blocks(owners, pos_ref, blocks_ref, order_ref, got_ref, starts_ref, acc_ref)
        out_ref[...] = acc_ref[...].reshape(out_ref.shape).astype(jnp.bfloat16)

    weight_ref[...] = half_weights(resp_in_ref, resp_grad_ref, prompt_in_ref, out_ref[...])


def join_kernel(
    owners, pos_ref, blocks_ref, order_ref, got_ref, value_ref, out_ref, starts_ref, acc_ref
):
    sum_blocks(owners, pos_ref, blocks_ref, order_ref, got_ref, starts_ref, acc_ref)
    out_ref[:, :HD] = acc_ref[...].reshape(value_ref.shape).astype(jnp.bfloat16)
    out_ref[:, HD:] = value_ref[...]


def weight_kernel(
    pos_ref, resp_in_ref, resp_grad_ref, prompt_in_ref, prompt_grad_ref, weight_ref
):
    weight_ref[...] = half_weights(
        resp_in_ref, resp_grad_ref, prompt_in_ref, prompt_grad_ref[...]
    )


def finish_kernel(pos_ref, mine_ref, theirs_ref, out_hbm, sems):
    half = mine_ref.shape[0]
    core = pos_ref[0] & 1
    copies = [
        pltpu.make_async_copy(
            source, out_hbm.at[pl.ds(pl.multiple_of(place * half, half), half)], sems.at[i]
        )
        for i, (source, place) in enumerate(((mine_ref, core), (theirs_ref, 1 - core)))
    ]
    for copy in copies:
        copy.start()
    for copy in copies:
        copy.wait()


def smem():
    return pl.BlockSpec(memory_space=pltpu.SMEM)


def vmem():
    return pl.BlockSpec(memory_space=pltpu.VMEM)


def hbm():
    return pl.BlockSpec(memory_space=pltpu.HBM)


def in_hbm(x):
    return pltpu.with_memory_space_constraint(x, pltpu.HBM)


def params():
    return pltpu.CompilerParams(vmem_limit_bytes=20 * 1024 * 1024)


def grp_sum(part, grp_count):
    total, step = part, 1
    while step < grp_count:
        width = min(4, grp_count // step)
        own = total.astype(jnp.bfloat16)
        terms = [own.astype(jnp.float32)]
        for k in range(1, width):
            pairs = [(i, i ^ (k * step)) for i in range(grp_count)]
            terms.append(lax.ppermute(own, "grp", pairs).astype(jnp.float32))
        while len(terms) > 1:
            terms = [terms[i] + terms[i + 1] for i in range(0, len(terms), 2)]
        total, step = terms[0], step * width
    return total


def local(
    queries,
    resp_kv,
    grad_out,
    prompt_kv,
    resp_inputs,
    prompt_inputs,
    prompt_blocks,
    response_order,
    response_len,
):
    bf16, f32 = jnp.bfloat16, jnp.float32
    owners = lax.axis_size("seq")
    grp_count = lax.axis_size("grp")
    slot_rows = prompt_kv.shape[1]
    responses = owners * RESP_DEV
    pos = lax.axis_index("seq").astype(jnp.int32).reshape(1)
    blocks, order, lengths = prompt_blocks[0], response_order[0], response_len[0]

    packed = pl.pallas_call(
        functools.partial(pack_kernel, owners),
        out_shape=jax.ShapeDtypeStruct((responses, PB, 2 * HD), bf16),
        in_specs=[smem()] + [hbm()] * 3,
        out_specs=vmem(),
        scratch_shapes=[
            pltpu.SMEM(blocks.shape, jnp.int32),
            pltpu.SMEM(order.shape, jnp.int32),
            pltpu.SMEM(blocks.shape, jnp.int32),
            pltpu.VMEM(prompt_kv.shape[1:2] + (PB, 2 * HD), bf16),
            pltpu.SemaphoreType.DMA((3,)),
        ],
        compiler_params=params(),
        name="pack",
    )(pos, in_hbm(prompt_blocks), in_hbm(response_order), in_hbm(prompt_kv))
    fetched = lax.all_to_all(
        packed.reshape(responses * PB, 2 * HD), "seq", 0, 0, tiled=True
    ).reshape(owners, RESP_DEV, PB, 2 * HD)

    keys = owners * PB + RLEN
    part_shape = jax.ShapeDtypeStruct((owners, RESP_DEV, PB, HD), bf16)
    down_v, part_v, score_grad = pl.pallas_call(
        functools.partial(attention_kernel, owners),
        out_shape=(
            jax.ShapeDtypeStruct((RESP_DEV * RLEN, HD), bf16),
            part_shape,
            pltpu.HBM((RESP_DEV, keys, ROWS), bf16),
        ),
        in_specs=[smem()] * 4 + [vmem()] * 4,
        out_specs=[vmem(), vmem(), hbm()],
        scratch_shapes=[
            pltpu.VMEM((keys, ROWS), f32),
            pltpu.VMEM((keys, ROWS), f32),
            pltpu.VMEM((RESP_DEV, keys, ROWS), bf16),
            pltpu.SemaphoreType.DMA((RESP_DEV,)),
        ],
        compiler_params=params(),
        name="attention",
    )(pos, blocks, order, lengths, queries[0], resp_kv[0], grad_out[0], fetched)

    def to_owners(part):
        got = lax.all_to_all(part.reshape(responses * PB, HD), "seq", 0, 0, tiled=True)
        return got.reshape(responses, PB, HD)

    returned_v = to_owners(part_v)
    d_queries, d_resp_kv, part_k = pl.pallas_call(
        functools.partial(query_key_kernel, owners),
        out_shape=(
            jax.ShapeDtypeStruct((RESP_DEV * RLEN, HEADS * HD), bf16),
            jax.ShapeDtypeStruct((RESP_DEV * RLEN, 2 * HD), bf16),
            part_shape,
        ),
        in_specs=[vmem(), vmem(), vmem(), hbm(), vmem()],
        out_specs=[vmem()] * 3,
        scratch_shapes=[
            pltpu.VMEM((RESP_DEV, keys, ROWS), bf16),
            pltpu.SemaphoreType.DMA((RESP_DEV,)),
        ],
        compiler_params=params(),
        name="query_key",
    )(queries[0], resp_kv[0], fetched, in_hbm(score_grad), down_v)

    rows, prompt_rows = RESP_DEV * RLEN, slot_rows * PB
    width = resp_inputs.shape[2]
    half = width // 2
    steps = half // CHUNK
    resp_in = resp_inputs[0]
    prompt_in = prompt_inputs[0].reshape(prompt_rows, width)

    d_value, sent = pl.pallas_call(
        functools.partial(combine_kernel, owners),
        out_shape=(
            jax.ShapeDtypeStruct((prompt_rows, HD), bf16),
            jax.ShapeDtypeStruct((half, HD), bf16),
        ),
        grid_spec=pltpu.PrefetchScalarGridSpec(
            num_scalar_prefetch=3,
            grid=(steps,),
            in_specs=[
                pl.BlockSpec((responses, PB, HD), lambda i, *_: (0, 0, 0)),
                pl.BlockSpec((rows, CHUNK), lambda i, p, *_: (0, (1 - (p[0] & 1)) * steps + i)),
                pl.BlockSpec((rows, HD), lambda i, *_: (0, 0)),
                pl.BlockSpec(
                    (prompt_rows, CHUNK), lambda i, p, *_: (0, (1 - (p[0] & 1)) * steps + i)
                ),
            ],
            out_specs=[
                pl.BlockSpec((prompt_rows, HD), lambda i, *_: (0, 0)),
                pl.BlockSpec((CHUNK, HD), lambda i, *_: (i, 0)),
            ],
            scratch_shapes=[
                pltpu.SMEM((blocks.shape[0],), jnp.int32),
                pltpu.VMEM((slot_rows, PB, HD), f32),
            ],
        ),
        compiler_params=params(),
        name="combine",
    )(pos, blocks, order, returned_v, resp_in, down_v, prompt_in)
    swap = [(i, i ^ 1) for i in range(owners)]
    from_twin = lax.ppermute(sent, "seq", swap)
    kept = pl.pallas_call(
        weight_kernel,
        out_shape=jax.ShapeDtypeStruct((half, HD), bf16),
        grid_spec=pltpu.PrefetchScalarGridSpec(
            num_scalar_prefetch=1,
            grid=(steps,),
            in_specs=[
                pl.BlockSpec((rows, CHUNK), lambda i, p: (0, (p[0] & 1) * steps + i)),
                pl.BlockSpec((rows, HD), lambda i, p: (0, 0)),
                pl.BlockSpec((prompt_rows, CHUNK), lambda i, p: (0, (p[0] & 1) * steps + i)),
                pl.BlockSpec((prompt_rows, HD), lambda i, p: (0, 0)),
            ],
            out_specs=pl.BlockSpec((CHUNK, HD), lambda i, p: (i, 0)),
        ),
        compiler_params=params(),
        name="weights",
    )(pos, resp_in, down_v, prompt_in, d_value)

    both = (kept.astype(f32) + from_twin.astype(f32)).astype(bf16)
    twins = [list(range(c, owners, 2)) for c in range(2)]
    chips = owners // 2
    shares = lax.all_to_all(both, "seq", 0, 0, tiled=True, axis_index_groups=twins)
    share = jnp.sum(shares.reshape(chips, half // chips, HD).astype(f32), axis=0)
    share, part_k = lax.optimization_barrier((share, part_k))
    returned_k = to_owners(part_k)
    key_total = grp_count * owners * (rows + prompt_rows)
    share = (grp_sum(share, grp_count) * key_total ** (-0.5)).astype(bf16)
    share, returned_k = lax.optimization_barrier((share, returned_k))
    copies = jnp.broadcast_to(share[None], (chips,) + share.shape).reshape(half, HD)
    mine = lax.all_to_all(copies, "seq", 0, 0, tiled=True, axis_index_groups=twins)
    theirs = lax.ppermute(mine, "seq", swap)
    d_value_weight = pl.pallas_call(
        finish_kernel,
        out_shape=pltpu.HBM((width, HD), bf16),
        in_specs=[smem(), vmem(), vmem()],
        out_specs=hbm(),
        scratch_shapes=[pltpu.SemaphoreType.DMA((2,))],
        compiler_params=params(),
        name="finish",
    )(pos, mine, theirs)
    d_prompt = pl.pallas_call(
        functools.partial(join_kernel, owners),
        out_shape=jax.ShapeDtypeStruct((prompt_rows, 2 * HD), bf16),
        in_specs=[smem()] * 3 + [vmem()] * 2,
        out_specs=vmem(),
        scratch_shapes=[
            pltpu.SMEM(blocks.shape, jnp.int32),
            pltpu.VMEM((slot_rows, PB, HD), f32),
        ],
        compiler_params=params(),
        name="join",
    )(pos, blocks, order, returned_k, d_value)
    d_prompt = d_prompt.reshape(slot_rows, PB, 2 * HD)
    return (d_queries[None], d_resp_kv[None], d_prompt[None], d_value_weight)


def solution(mesh):
    in_specs = (
        P("grp", "seq", None),
        P("grp", "seq", None),
        P("grp", "seq", None),
        P("grp", None, "seq", None),
        P("grp", "seq", None),
        P("grp", None, "seq", None),
        P("grp", None),
        P("grp", None),
        P("grp", "seq"),
    )
    out_specs = (P("grp", "seq", None), P("grp", "seq", None), P("grp", None, "seq", None), P())
    return jax.shard_map(local, mesh=mesh, in_specs=in_specs, out_specs=out_specs, check_vma=False)
```

time: 159 us -> 134 us (0.84)
  blocking collectives: 120 us -> 73.8 us
  waiting for transfers between devices: 4.83 us -> 16.4 us
  starting transfers between devices: 10.7 us -> 21.9 us
  Pallas kernels: 11.2 us -> 19.4 us
  local copies, waits for them, and re-layouts: 6.08 us -> 0.14 us
  matrix products: 3.45 us -> 0 us
    all_to_all x3 -> x2, blocking collectives: 82.8 us -> 36.9 us  [the longest x1 20.8 us: to_owners(): lax.all_to_all(part.reshape(responses * PB, HD), 'seq', 0, 0, tiled=True)]
    pallas_call x1 -> x5, Pallas kernels: 2.39 us -> 11.7 us  [the longest x1 4.34 us: local(): pl.pallas_call(functools.partial(query_key_kernel, owners), out_shape=(ja...]
    all_to_all x0 -> x2, waiting for transfers between devices: none -> 8.58 us  [the longest x1 8.14 us: local(): lax.all_to_all(both, 'seq', 0, 0, tiled=True, axis_index_groups=twins)]
    all_to_all x0 -> x2, starting transfers between devices: none -> 8.56 us  [the longest x1 4.97 us: to_owners(): lax.all_to_all(part.reshape(responses * PB, HD), 'seq', 0, 0, tiled=True)]
    dot_general x2 -> x0, matrix products: 3.45 us -> none  [the longest x1 1.87 us: local(): jnp.einsum('std,stk->dk', prompt_inputs[0], d_prompt[:, :, HD:], preferre...]
    unnamed x21 -> x16, local copies, waits for them, and re-layouts: 3.47 us -> 0.05 us
    ppermute x4 -> x6, waiting for transfers between devices: 4.83 us -> 7.85 us  [the longest x4 7.79 us: grp_sum(): terms.append(lax.ppermute(own, 'grp', pairs).astype(jnp.float32))]
    ppermute x4 -> x6, starting transfers between devices: 10.7 us -> 13.3 us  [the longest x4 9.01 us: grp_sum(): terms.append(lax.ppermute(own, 'grp', pairs).astype(jnp.float32))]
  transfers between devices with their start and end apart: 4 -> 8, of which waited for: 3 -> 6; matrix products, arithmetic and copies ran while one was open for 0% -> 0% of each run, Pallas kernels for 0% -> 6%
where the time goes in v2:
time: 134 us
  blocking collectives  73.8 us (55%)
  starting transfers between devices  21.9 us (16%)
  Pallas kernels  19.4 us (14%)
  waiting for transfers between devices  16.4 us (12%)
    all_to_all x1, blocking collectives, local(): lax.all_to_all(packed.reshape(responses * PB, 2 * HD), 'seq', 0, 0, tiled...  36.9 us
    all_to_all x1, blocking collectives, to_owners(): lax.all_to_all(part.reshape(responses * PB, HD), 'seq', 0, 0, tiled=True)  20.8 us
    all_to_all x1, blocking collectives, local(): lax.all_to_all(copies, 'seq', 0, 0, tiled=True, axis_index_groups=twins)  16.1 us
    ppermute x4, starting transfers between devices, grp_sum(): terms.append(lax.ppermute(own, 'grp', pairs).astype(jnp.float32))  9.01 us
    all_to_all x1, waiting for transfers between devices, local(): lax.all_to_all(both, 'seq', 0, 0, tiled=True, axis_index_groups=twins)  8.14 us
    ppermute x4, waiting for transfers between devices, grp_sum(): terms.append(lax.ppermute(own, 'grp', pairs).astype(jnp.float32))  7.79 us
    pallas_call x1, Pallas kernels, local(): pl.pallas_call(functools.partial(attention_kernel, owners), out_shape=(ja...  6.53 us
    all_to_all x1, starting transfers between devices, to_owners(): lax.all_to_all(part.reshape(responses * PB, HD), 'seq', 0, 0, tiled=True)  4.97 us
  transfers between devices with their start and end apart: 8, of which 6 were waited for; matrix products, arithmetic and copies ran while one was open for 0% of the time, Pallas kernels for 6%

profile of v2, /device:TPU:1, one launch (start us, length us, event | category | flops | bytes accessed | tf_op | source)
XLA Modules:
  0.0 133.7 jit_solution(17244491879930430975)
XLA Ops:
  0.6 1.2 pack.1
  1.9 36.9 %all_to_all.44 = bf16[32,128,256]{2,1,0:T(8,128)(2,1)S(1)} all-to-all(bf16[32,128,256]{2,1,0:T(8,128)(2,1)S(1)} %bitcast.24), channel_id=1, replica_groups=mesh['grp'=8,'seq'=32] {'seq'}, dimensions={0} | all-to-all | bytes 4194304 | tf_op jit(solution)/shard_map/all_to_all | solution.py:354
  38.9 6.5 %attention.1 = (bf16[128,128]{1,0:T(8,128)(2,1)S(1)}, bf16[32,2,64,128]{3,2,1,0:T(8,128)(2,1)S(1)}, bf16[2,2112,320]{2,1,0:T(8,128)(2,1)}) custom-call(s32[1]{0:T(128)} %bitcast.2.pos_ref, s32[8]{0:T(128)S(1)} %bitcast.37, s32[64]{0:T(128)S(1)} %bitcast.40, s32[2]{0:T(128)S(1)} %bitcast.43, bf16[128,640]{1,0:T(8,128)(2,1)S(1)} %bitcast.32, ...), custom_call_target="tpu_custom_call" | custom-call | tf_op jit(solution)/shard_map/attention/pallas_call | solution.py:360
  45.4 20.8 %all_to_all.45 = bf16[32,128,128]{2,1,0:T(8,128)(2,1)S(1)} all-to-all(bf16[32,128,128]{2,1,0:T(8,128)(2,1)S(1)} %bitcast.31), channel_id=1, replica_groups=mesh['grp'=8,'seq'=32] {'seq'}, dimensions={0} | all-to-all | bytes 2097152 | tf_op jit(solution)/shard_map/all_to_all | solution.py:380
  66.3 2.8 %combine.1 = (bf16[320,128]{1,0:T(8,128)(2,1)S(1)}, bf16[2560,128]{1,0:T(8,128)(2,1)S(1)}) custom-call(s32[1]{0:T(128)} %bitcast.2.pos_ref, s32[8]{0:T(128)S(1)} %bitcast.38, s32[64]{0:T(128)S(1)} %bitcast.41, bf16[64,64,128]{2,1,0:T(8,128)(2,1)S(1)} %bitcast.27, bf16[128,5120]{1,0:T(8,128)(2,1)S(1)} %bitcast.25, ...), custom_call_target="tpu_custom_call" | custom-call | tf_op jit(solution)/shard_map/combine/pallas_call | solution.py:408
  69.1 0.5 collective-permute-start
  69.6 1.8 %weights.1 = bf16[2560,128]{1,0:T(8,128)(2,1)S(1)} custom-call(s32[1]{0:T(128)} %bitcast.2.pos_ref, bf16[128,5120]{1,0:T(8,128)(2,1)S(1)} %bitcast.26, bf16[128,128]{1,0:T(8,128)(2,1)S(1)} %get-tuple-element.17.down_v_ref.resp_grad_ref, bf16[320,5120]{1,0:T(8,128)(2,1)S(1)} %bitcast.23, bf16[320,128]{1,0:T(8,128)(2,1)S(1)} %get-tuple-element.21.prompt_grad_ref.value_ref), custom_call_target="tpu_custom_call" | custom-call | tf_op jit(solution)/shard_map/weights/pallas_call | solution.py:439
  71.4 1.0 add_convert_fusion
  72.5 3.6 %all-to-all-start.2 = ((bf16[16,160,128]{2,1,0:T(8,128)(2,1)}), bf16[16,160,128]{2,1,0:T(8,128)(2,1)S(1)}, u32[]{:S(2)}, u32[]{:S(2)}) async-start(bf16[16,160,128]{2,1,0:T(8,128)(2,1)} %bitcast.44), calls=%async_computation.2 | async-start | bytes 1310720 | tf_op jit(solution)/shard_map/all_to_all | solution.py:460
  76.1 4.3 %query_key.1 = (bf16[128,640]{1,0:T(8,128)(2,1)}, bf16[128,256]{1,0:T(8,128)(2,1)}, bf16[32,2,64,128]{3,2,1,0:T(8,128)(2,1)}) custom-call(bf16[128,640]{1,0:T(8,128)(2,1)S(1)} %bitcast.33, bf16[128,256]{1,0:T(8,128)(2,1)S(1)} %bitcast.35, bf16[32,2,64,256]{3,2,1,0:T(8,128)(2,1)S(1)} %bitcast.21, bf16[2,2112,320]{2,1,0:T(8,128)(2,1)} %get-tuple-element.16.sgrad_hbm, ...), custom_call_target="tpu_custom_call" | custom-call | tf_op jit(solution)/shard_map/query_key/pallas_call | solution.py:384
  80.4 8.1 %all-to-all-done.2 = bf16[16,160,128]{2,1,0:T(8,128)(2,1)S(1)} async-done(((bf16[16,160,128]{2,1,0:T(8,128)(2,1)}), bf16[16,160,128]{2,1,0:T(8,128)(2,1)S(1)}, u32[]{:S(2)}, u32[]{:S(2)}) %all-to-all-start.2) | async-done | bytes 655392 | tf_op jit(solution)/shard_map/all_to_all | solution.py:460
  88.5 0.1 convert_reduce_fusion
  88.6 5.0 %all-to-all-start.3 = ((bf16[32,128,128]{2,1,0:T(8,128)(2,1)}), bf16[32,128,128]{2,1,0:T(8,128)(2,1)S(1)}, u32[]{:S(2)}, u32[]{:S(2)}) async-start(bf16[32,128,128]{2,1,0:T(8,128)(2,1)} %bitcast.16), calls=%async_computation.3 | async-start | bytes 2097152 | tf_op jit(solution)/shard_map/all_to_all | solution.py:380
  93.6 1.7 %collective-permute-start.1 = (bf16[160,128]{1,0:T(8,128)(2,1)S(1)}, bf16[160,128]{1,0:T(8,128)(2,1)S(1)}, u32[]{:S(2)}, u32[]{:S(2)}) collective-permute-start(bf16[160,128]{1,0:T(8,128)(2,1)S(1)} %convert_reduce_fusion), channel_id=1, source_target_pairs={{0,32},{32,0},{64,96},{96,64},{128,160},{160,128},{192,224},{224,1... | collective-permute-start | bytes 122888 | tf_op jit(solution)/shard_map/ppermute | solution.py:313
  95.3 3.0 %collective-permute-start.2 = (bf16[160,128]{1,0:T(8,128)(2,1)S(1)}, bf16[160,128]{1,0:T(8,128)(2,1)S(1)}, u32[]{:S(2)}, u32[]{:S(2)}) collective-permute-start(bf16[160,128]{1,0:T(8,128)(2,1)S(1)} %convert_reduce_fusion), channel_id=1, source_target_pairs={{0,64},{32,96},{64,0},{96,32},{128,192},{160,224},{192,128},{224,1... | collective-permute-start | bytes 122888 | tf_op jit(solution)/shard_map/ppermute | solution.py:313
  98.3 2.2 %collective-permute-done.2 = bf16[160,128]{1,0:T(8,128)(2,1)S(1)} collective-permute-done((bf16[160,128]{1,0:T(8,128)(2,1)S(1)}, bf16[160,128]{1,0:T(8,128)(2,1)S(1)}, u32[]{:S(2)}, u32[]{:S(2)}) %collective-permute-start.2) | collective-permute-done | bytes 40992 | tf_op jit(solution)/shard_map/ppermute | solution.py:313
  100.5 2.8 %collective-permute-done.3 = bf16[160,128]{1,0:T(8,128)(2,1)S(1)} collective-permute-done((bf16[160,128]{1,0:T(8,128)(2,1)S(1)}, bf16[160,128]{1,0:T(8,128)(2,1)S(1)}, u32[]{:S(2)}, u32[]{:S(2)}) %collective-permute-start.3) | collective-permute-done | bytes 40992 | tf_op jit(solution)/shard_map/ppermute | solution.py:313
  103.3 4.3 %collective-permute-start.4 = (bf16[160,128]{1,0:T(8,128)(2,1)S(1)}, bf16[160,128]{1,0:T(8,128)(2,1)S(1)}, u32[]{:S(2)}, u32[]{:S(2)}) collective-permute-start(bf16[160,128]{1,0:T(8,128)(2,1)S(1)} %add_convert_fusion.1), channel_id=1, source_target_pairs={{0,128},{32,160},{64,192},{96,224},{128,0},{160,32},{192,64},{224,... | collective-permute-start | bytes 122888 | tf_op jit(solution)/shard_map/ppermute | solution.py:313
  107.6 2.8 %collective-permute-done.4 = bf16[160,128]{1,0:T(8,128)(2,1)S(1)} collective-permute-done((bf16[160,128]{1,0:T(8,128)(2,1)S(1)}, bf16[160,128]{1,0:T(8,128)(2,1)S(1)}, u32[]{:S(2)}, u32[]{:S(2)}) %collective-permute-start.4) | collective-permute-done | bytes 40992 | tf_op jit(solution)/shard_map/ppermute | solution.py:313
  110.5 0.4 all-to-all-done.3
  111.0 16.1 %all_to_all.46 = bf16[16,160,128]{2,1,0:T(8,128)(2,1)S(1)} all-to-all(bf16[16,160,128]{2,1,0:T(8,128)(2,1)S(1)} %broadcast_in_dim.14), channel_id=1, replica_groups={{0,2,4,6,8,10,12,14,16,18,20,22,24,26,28,30},{1,3,5,7,9,11,13,15,17,19,..., dimensions={0} | all-to-all | bytes 1310720 | tf_op jit(solution)/shard_map/all_to_all | solution.py:468
  127.0 3.8 %collective-permute-start.5 = (bf16[2560,128]{1,0:T(8,128)(2,1)S(1)}, bf16[2560,128]{1,0:T(8,128)(2,1)S(1)}, u32[]{:S(2)}, u32[]{:S(2)}) collective-permute-start(bf16[2560,128]{1,0:T(8,128)(2,1)S(1)} %bitcast.29), channel_id=1, source_target_pairs={{0,1},{1,0},{2,3},{3,2},{4,5},{5,4},{6,7},{7,6},{8,9},{9,8},{10,11... | collective-permute-start | bytes 1966088 | tf_op jit(solution)/shard_map/ppermute | solution.py:469
  130.9 1.7 %join.1 = bf16[320,256]{1,0:T(8,128)(2,1)} custom-call(s32[1]{0:T(128)} %bitcast.2.pos_ref, s32[8]{0:T(128)S(1)} %bitcast.39, s32[64]{0:T(128)S(1)} %bitcast.42, bf16[64,64,128]{2,1,0:T(8,128)(2,1)S(1)} %bitcast.28, bf16[320,128]{1,0:T(8,128)(2,1)S(1)} %get-tuple-element.21.prompt_grad_ref.value_ref), custom_call_target="tpu_custom_call" | custom-call | tf_op jit(solution)/shard_map/join/pallas_call | solution.py:479
  132.6 1.1 finish.1
  (23 shorter events, 0.2 us)
Async XLA Ops:
  1.8 37.0 %copy-start.2 = (bf16[1,128,640]{2,1,0:T(8,128)(2,1)S(1)}, bf16[1,128,640]{2,1,0:T(8,128)(2,1)}, u32[]{:S(2)}) copy-start(bf16[1,128,640]{2,1,0:T(8,128)(2,1)} %param.9) | copy-start | bytes 491524
  1.9 37.0 %copy-start.3 = (bf16[1,128,256]{2,1,0:T(8,128)(2,1)S(1)}, bf16[1,128,256]{2,1,0:T(8,128)(2,1)}, u32[]{:S(2)}) copy-start(bf16[1,128,256]{2,1,0:T(8,128)(2,1)} %param.10) | copy-start | bytes 196612
  1.9 37.0 %copy-start.4 = (bf16[1,128,640]{2,1,0:T(8,128)(2,1)S(1)}, bf16[1,128,640]{2,1,0:T(8,128)(2,1)}, u32[]{:S(2)}) copy-start(bf16[1,128,640]{2,1,0:T(8,128)(2,1)} %param.11) | copy-start | bytes 491524
  1.9 37.0 %copy-start.5 = (s32[1,8]{1,0:T(1,128)S(1)}, s32[1,8]{1,0:T(1,128)}, u32[]{:S(2)}) copy-start(s32[1,8]{1,0:T(1,128)} %blocks_hbm.1) | copy-start | bytes 100
  1.9 37.0 %copy-start.6 = (s32[1,64]{1,0:T(1,128)S(1)}, s32[1,64]{1,0:T(1,128)}, u32[]{:S(2)}) copy-start(s32[1,64]{1,0:T(1,128)} %order_hbm.1) | copy-start | bytes 772
  1.9 37.0 %copy-start.7 = (s32[1,2]{1,0:T(1,128)S(1)}, s32[1,2]{1,0:T(1,128)}, u32[]{:S(2)}) copy-start(s32[1,2]{1,0:T(1,128)} %param.17) | copy-start | bytes 28
  38.9 27.4 %copy-start = (bf16[1,5,64,5120]{3,2,1,0:T(8,128)(2,1)S(1)}, bf16[1,5,64,5120]{3,2,1,0:T(8,128)(2,1)}, u32[]{:S(2)}) copy-start(bf16[1,5,64,5120]{3,2,1,0:T(8,128)(2,1)} %param.14) | copy-start | bytes 9830404
  45.4 20.8 %copy-start.1 = (bf16[1,128,5120]{2,1,0:T(8,128)(2,1)S(1)}, bf16[1,128,5120]{2,1,0:T(8,128)(2,1)}, u32[]{:S(2)}) copy-start(bf16[1,128,5120]{2,1,0:T(8,128)(2,1)} %param.13) | copy-start | bytes 3932164
  69.1 2.3 %collective-permute-start = (bf16[2560,128]{1,0:T(8,128)(2,1)S(1)}, bf16[2560,128]{1,0:T(8,128)(2,1)S(1)}, u32[]{:S(2)}, u32[]{:S(2)}) collective-permute-start(bf16[2560,128]{1,0:T(8,128)(2,1)S(1)} %get-tuple-element.22), channel_id=1, source_target_pairs={{0,1},{1,0},{2,3},{3,2},{4,5},{5,4},{6,7},{7,6},{8,9},{9,8},{10,11... | collective-permute-start | bytes 1966088 | tf_op jit(solution)/shard_map/ppermute | solution.py:438
  72.5 16.1 %all-to-all-start.2 = ((bf16[16,160,128]{2,1,0:T(8,128)(2,1)}), bf16[16,160,128]{2,1,0:T(8,128)(2,1)S(1)}, u32[]{:S(2)}, u32[]{:S(2)}) async-start(bf16[16,160,128]{2,1,0:T(8,128)(2,1)} %bitcast.44), calls=%async_computation.2 | async-start | bytes 1310720 | tf_op jit(solution)/shard_map/all_to_all | solution.py:460
  88.6 22.3 %all-to-all-start.3 = ((bf16[32,128,128]{2,1,0:T(8,128)(2,1)}), bf16[32,128,128]{2,1,0:T(8,128)(2,1)S(1)}, u32[]{:S(2)}, u32[]{:S(2)}) async-start(bf16[32,128,128]{2,1,0:T(8,128)(2,1)} %bitcast.16), calls=%async_computation.3 | async-start | bytes 2097152 | tf_op jit(solution)/shard_map/all_to_all | solution.py:380
  93.6 4.7 %collective-permute-start.1 = (bf16[160,128]{1,0:T(8,128)(2,1)S(1)}, bf16[160,128]{1,0:T(8,128)(2,1)S(1)}, u32[]{:S(2)}, u32[]{:S(2)}) collective-permute-start(bf16[160,128]{1,0:T(8,128)(2,1)S(1)} %convert_reduce_fusion), channel_id=1, source_target_pairs={{0,32},{32,0},{64,96},{96,64},{128,160},{160,128},{192,224},{224,1... | collective-permute-start | bytes 122888 | tf_op jit(solution)/shard_map/ppermute | solution.py:313
  95.3 5.2 %collective-permute-start.2 = (bf16[160,128]{1,0:T(8,128)(2,1)S(1)}, bf16[160,128]{1,0:T(8,128)(2,1)S(1)}, u32[]{:S(2)}, u32[]{:S(2)}) collective-permute-start(bf16[160,128]{1,0:T(8,128)(2,1)S(1)} %convert_reduce_fusion), channel_id=1, source_target_pairs={{0,64},{32,96},{64,0},{96,32},{128,192},{160,224},{192,128},{224,1... | collective-permute-start | bytes 122888 | tf_op jit(solution)/shard_map/ppermute | solution.py:313
  98.3 4.9 %collective-permute-start.3 = (bf16[160,128]{1,0:T(8,128)(2,1)S(1)}, bf16[160,128]{1,0:T(8,128)(2,1)S(1)}, u32[]{:S(2)}, u32[]{:S(2)}) collective-permute-start(bf16[160,128]{1,0:T(8,128)(2,1)S(1)} %convert_reduce_fusion), channel_id=1, source_target_pairs={{0,96},{32,64},{64,32},{96,0},{128,224},{160,192},{192,160},{224,1... | collective-permute-start | bytes 122888 | tf_op jit(solution)/shard_map/ppermute | solution.py:313
  103.3 7.1 %collective-permute-start.4 = (bf16[160,128]{1,0:T(8,128)(2,1)S(1)}, bf16[160,128]{1,0:T(8,128)(2,1)S(1)}, u32[]{:S(2)}, u32[]{:S(2)}) collective-permute-start(bf16[160,128]{1,0:T(8,128)(2,1)S(1)} %add_convert_fusion.1), channel_id=1, source_target_pairs={{0,128},{32,160},{64,192},{96,224},{128,0},{160,32},{192,64},{224,... | collective-permute-start | bytes 122888 | tf_op jit(solution)/shard_map/ppermute | solution.py:313
  127.0 5.6 %collective-permute-start.5 = (bf16[2560,128]{1,0:T(8,128)(2,1)S(1)}, bf16[2560,128]{1,0:T(8,128)(2,1)S(1)}, u32[]{:S(2)}, u32[]{:S(2)}) collective-permute-start(bf16[2560,128]{1,0:T(8,128)(2,1)S(1)} %bitcast.29), channel_id=1, source_target_pairs={{0,1},{1,0},{2,3},{3,2},{4,5},{5,4},{6,7},{7,6},{8,9},{9,8},{10,11... | collective-permute-start | bytes 1966088 | tf_op jit(solution)/shard_map/ppermute | solution.py:469

commit v3 on v2

--- a/solution.py
+++ b/solution.py
@@ -125,11 +125,15 @@
             else:
                 k = own_ref[rows, :HD]
             s = lax.dot_general(k, q, NT, preferred_element_type=f32)
-            key_ids = lax.broadcasted_iota(jnp.int32, s.shape, 0)
             if i < chunks:
-                offset = ((key_ids >> 6) + (i * OWN_BLOCKS - begin)) & (owners - 1)
-                s = jnp.where(offset < count, s, -1e30)
+                seen = []
+                for j in range(OWN_BLOCKS):
+                    offset = (i * OWN_BLOCKS + j - begin) & (owners - 1)
+                    hidden = jnp.where(offset < count, 0.0, -1e30)
+                    seen.append(s[j * PB : (j + 1) * PB] + hidden)
+                s = jnp.concatenate(seen, axis=0)
             else:
+                key_ids = lax.broadcasted_iota(jnp.int32, s.shape, 0)
                 query_ids = lax.broadcasted_iota(jnp.int32, s.shape, 1) & (RLEN - 1)
                 s = jnp.where(key_ids <= query_ids, s, -1e30)
             score_ref[rows_of(i), :] = s
@@ -209,11 +213,17 @@
     down_ref[:, HD:] = down_v_ref[...]
 
 
-def half_weights(resp_in_ref, resp_grad_ref, prompt_in_ref, prompt_grad):
-    f32 = jnp.float32
-    term = lax.dot_general(resp_in_ref[...], resp_grad_ref[...], TN, preferred_element_type=f32)
-    more = lax.dot_general(prompt_in_ref[...], prompt_grad, TN, preferred_element_type=f32)
-    return (term + more).astype(jnp.bfloat16)
+def half_weights(core, resp_in_ref, resp_grad, prompt_in_ref, prompt_grad, weight_ref):
+    half = weight_ref.shape[0]
+    for i in range(half // CHUNK):
+        place = pl.ds(pl.multiple_of(core * half + i * CHUNK, HD), CHUNK)
+        term = lax.dot_general(
+            resp_in_ref[:, place], resp_grad, TN, preferred_element_type=jnp.float32
+        )
+        more = lax.dot_general(
+            prompt_in_ref[:, place], prompt_grad, TN, preferred_element_type=jnp.float32
+        )
+        weight_ref[i * CHUNK : (i + 1) * CHUNK, :] = (term + more).astype(jnp.bfloat16)
 
 
 def sum_blocks(owners, pos_ref, blocks_ref, order_ref, got_ref, starts_ref, acc_ref):
@@ -243,12 +253,11 @@
     starts_ref,
     acc_ref,
 ):
-    @pl.when(pl.program_id(0) == 0)
-    def _():
-        sum_blocks(owners, pos_ref, blocks_ref, order_ref, got_ref, starts_ref, acc_ref)
-        out_ref[...] = acc_ref[...].reshape(out_ref.shape).astype(jnp.bfloat16)
-
-    weight_ref[...] = half_weights(resp_in_ref, resp_grad_ref, prompt_in_ref, out_ref[...])
+    sum_blocks(owners, pos_ref, blocks_ref, order_ref, got_ref, starts_ref, acc_ref)
+    prompt_grad = acc_ref[...].reshape(out_ref.shape).astype(jnp.bfloat16)
+    out_ref[...] = prompt_grad
+    other = 1 - (pos_ref[0] & 1)
+    half_weights(other, resp_in_ref, resp_grad_ref[...], prompt_in_ref, prompt_grad, weight_ref)
 
 
 def join_kernel(
@@ -262,8 +271,13 @@
 def weight_kernel(
     pos_ref, resp_in_ref, resp_grad_ref, prompt_in_ref, prompt_grad_ref, weight_ref
 ):
-    weight_ref[...] = half_weights(
-        resp_in_ref, resp_grad_ref, prompt_in_ref, prompt_grad_ref[...]
+    half_weights(
+        pos_ref[0] & 1,
+        resp_in_ref,
+        resp_grad_ref[...],
+        prompt_in_ref,
+        prompt_grad_ref[...],
+        weight_ref,
     )
 
 
@@ -401,7 +415,6 @@
     rows, prompt_rows = RESP_DEV * RLEN, slot_rows * PB
     width = resp_inputs.shape[2]
     half = width // 2
-    steps = half // CHUNK
     resp_in = resp_inputs[0]
     prompt_in = prompt_inputs[0].reshape(prompt_rows, width)
 
@@ -411,26 +424,12 @@
             jax.ShapeDtypeStruct((prompt_rows, HD), bf16),
             jax.ShapeDtypeStruct((half, HD), bf16),
         ),
-        grid_spec=pltpu.PrefetchScalarGridSpec(
-            num_scalar_prefetch=3,
-            grid=(steps,),
-            in_specs=[
-                pl.BlockSpec((responses, PB, HD), lambda i, *_: (0, 0, 0)),
-                pl.BlockSpec((rows, CHUNK), lambda i, p, *_: (0, (1 - (p[0] & 1)) * steps + i)),
-                pl.BlockSpec((rows, HD), lambda i, *_: (0, 0)),
-                pl.BlockSpec(
-                    (prompt_rows, CHUNK), lambda i, p, *_: (0, (1 - (p[0] & 1)) * steps + i)
-                ),
-            ],
-            out_specs=[
-                pl.BlockSpec((prompt_rows, HD), lambda i, *_: (0, 0)),
-                pl.BlockSpec((CHUNK, HD), lambda i, *_: (i, 0)),
-            ],
-            scratch_shapes=[
-                pltpu.SMEM((blocks.shape[0],), jnp.int32),
-                pltpu.VMEM((slot_rows, PB, HD), f32),
-            ],
-        ),
+        in_specs=[smem()] * 3 + [vmem()] * 4,
+        out_specs=[vmem()] * 2,
+        scratch_shapes=[
+            pltpu.SMEM((blocks.shape[0],), jnp.int32),
+            pltpu.VMEM((slot_rows, PB, HD), f32),
+        ],
         compiler_params=params(),
         name="combine",
     )(pos, blocks, order, returned_v, resp_in, down_v, prompt_in)
@@ -439,17 +438,8 @@
     kept = pl.pallas_call(
         weight_kernel,
         out_shape=jax.ShapeDtypeStruct((half, HD), bf16),
-        grid_spec=pltpu.PrefetchScalarGridSpec(
-            num_scalar_prefetch=1,
-            grid=(steps,),
-            in_specs=[
-                pl.BlockSpec((rows, CHUNK), lambda i, p: (0, (p[0] & 1) * steps + i)),
-                pl.BlockSpec((rows, HD), lambda i, p: (0, 0)),
-                pl.BlockSpec((prompt_rows, CHUNK), lambda i, p: (0, (p[0] & 1) * steps + i)),
-                pl.BlockSpec((prompt_rows, HD), lambda i, p: (0, 0)),
-            ],
-            out_specs=pl.BlockSpec((CHUNK, HD), lambda i, p: (i, 0)),
-        ),
+        in_specs=[smem()] + [vmem()] * 4,
+        out_specs=vmem(),
         compiler_params=params(),
         name="weights",
     )(pos, resp_in, down_v, prompt_in, d_value)

time: 134 us -> 133 us (level)
  Pallas kernels: 19.4 us -> 17.4 us
  transfers between devices with their start and end apart: 8 -> 8, of which waited for: 6 -> 7; matrix products, arithmetic and copies ran while one was open for 0% -> 0% of each run, Pallas kernels for 6% -> 5%
where the time goes in v3:
time: 133 us; the launch traced here: 132 us
  blocking collectives  73.8 us (55%)
  starting transfers between devices  22 us (17%)
  Pallas kernels  17.4 us (13%)
  waiting for transfers between devices  17.1 us (13%)
    all_to_all x1, blocking collectives, local(): lax.all_to_all(packed.reshape(responses * PB, 2 * HD), 'seq', 0, 0, tiled...  36.9 us
    all_to_all x1, blocking collectives, to_owners(): lax.all_to_all(part.reshape(responses * PB, HD), 'seq', 0, 0, tiled=True)  20.8 us
    all_to_all x1, blocking collectives, local(): lax.all_to_all(copies, 'seq', 0, 0, tiled=True, axis_index_groups=twins)  16 us
    ppermute x4, starting transfers between devices, grp_sum(): terms.append(lax.ppermute(own, 'grp', pairs).astype(jnp.float32))  9.01 us
    all_to_all x1, waiting for transfers between devices, local(): lax.all_to_all(both, 'seq', 0, 0, tiled=True, axis_index_groups=twins)  8.02 us
    ppermute x4, waiting for transfers between devices, grp_sum(): terms.append(lax.ppermute(own, 'grp', pairs).astype(jnp.float32))  7.78 us
    pallas_call x1, Pallas kernels, local(): pl.pallas_call(functools.partial(attention_kernel, owners), out_shape=(ja...  6.29 us
    all_to_all x1, starting transfers between devices, to_owners(): lax.all_to_all(part.reshape(responses * PB, HD), 'seq', 0, 0, tiled=True)  5.09 us
  transfers between devices with their start and end apart: 8, of which 7 were waited for; matrix products, arithmetic and copies ran while one was open for 0% of the time, Pallas kernels for 5%

profile of v3, /device:TPU:1, one launch (start us, length us, event | category | flops | bytes accessed | tf_op | source)
XLA Modules:
  0.0 132.4 jit_solution(10436789962247729461)
XLA Ops:
  0.6 1.2 pack.1
  1.9 36.9 %all_to_all.44 = bf16[32,128,256]{2,1,0:T(8,128)(2,1)S(1)} all-to-all(bf16[32,128,256]{2,1,0:T(8,128)(2,1)S(1)} %bitcast.24), channel_id=1, replica_groups=mesh['grp'=8,'seq'=32] {'seq'}, dimensions={0} | all-to-all | bytes 4194304 | tf_op jit(solution)/shard_map/all_to_all | solution.py:368
  38.9 6.3 %attention.1 = (bf16[128,128]{1,0:T(8,128)(2,1)S(1)}, bf16[32,2,64,128]{3,2,1,0:T(8,128)(2,1)S(1)}, bf16[2,2112,320]{2,1,0:T(8,128)(2,1)}) custom-call(s32[1]{0:T(128)} %bitcast.2.pos_ref, s32[8]{0:T(128)S(1)} %bitcast.37, s32[64]{0:T(128)S(1)} %bitcast.40, s32[2]{0:T(128)S(1)} %bitcast.43, bf16[128,640]{1,0:T(8,128)(2,1)S(1)} %bitcast.32, ...), custom_call_target="tpu_custom_call" | custom-call | tf_op jit(solution)/shard_map/attention/pallas_call | solution.py:374
  45.2 20.8 %all_to_all.45 = bf16[32,128,128]{2,1,0:T(8,128)(2,1)S(1)} all-to-all(bf16[32,128,128]{2,1,0:T(8,128)(2,1)S(1)} %bitcast.31), channel_id=1, replica_groups=mesh['grp'=8,'seq'=32] {'seq'}, dimensions={0} | all-to-all | bytes 2097152 | tf_op jit(solution)/shard_map/all_to_all | solution.py:394
  66.1 1.9 %combine.1 = (bf16[320,128]{1,0:T(8,128)(2,1)S(1)}, bf16[2560,128]{1,0:T(8,128)(2,1)S(1)}) custom-call(s32[1]{0:T(128)} %bitcast.2.pos_ref, s32[8]{0:T(128)S(1)} %bitcast.38, s32[64]{0:T(128)S(1)} %bitcast.41, bf16[64,64,128]{2,1,0:T(8,128)(2,1)S(1)} %bitcast.27, bf16[128,5120]{1,0:T(8,128)(2,1)S(1)} %bitcast.25, ...), custom_call_target="tpu_custom_call" | custom-call | tf_op jit(solution)/shard_map/combine/pallas_call | solution.py:421
  68.0 0.5 collective-permute-start
  68.5 0.9 weights.1
  69.4 0.8 collective-permute-done
  70.2 1.0 add_convert_fusion
  71.2 3.6 %all-to-all-start.2 = ((bf16[16,160,128]{2,1,0:T(8,128)(2,1)}), bf16[16,160,128]{2,1,0:T(8,128)(2,1)S(1)}, u32[]{:S(2)}, u32[]{:S(2)}) async-start(bf16[16,160,128]{2,1,0:T(8,128)(2,1)} %bitcast.44), calls=%async_computation.2 | async-start | bytes 1310720 | tf_op jit(solution)/shard_map/all_to_all | solution.py:450
  74.8 4.3 %query_key.1 = (bf16[128,640]{1,0:T(8,128)(2,1)}, bf16[128,256]{1,0:T(8,128)(2,1)}, bf16[32,2,64,128]{3,2,1,0:T(8,128)(2,1)}) custom-call(bf16[128,640]{1,0:T(8,128)(2,1)S(1)} %bitcast.33, bf16[128,256]{1,0:T(8,128)(2,1)S(1)} %bitcast.35, bf16[32,2,64,256]{3,2,1,0:T(8,128)(2,1)S(1)} %bitcast.21, bf16[2,2112,320]{2,1,0:T(8,128)(2,1)} %get-tuple-element.16.sgrad_hbm, ...), custom_call_target="tpu_custom_call" | custom-call | tf_op jit(solution)/shard_map/query_key/pallas_call | solution.py:398
  79.2 8.0 %all-to-all-done.2 = bf16[16,160,128]{2,1,0:T(8,128)(2,1)S(1)} async-done(((bf16[16,160,128]{2,1,0:T(8,128)(2,1)}), bf16[16,160,128]{2,1,0:T(8,128)(2,1)S(1)}, u32[]{:S(2)}, u32[]{:S(2)}) %all-to-all-start.2) | async-done | bytes 655392 | tf_op jit(solution)/shard_map/all_to_all | solution.py:450
  87.3 5.1 %all-to-all-start.3 = ((bf16[32,128,128]{2,1,0:T(8,128)(2,1)}), bf16[32,128,128]{2,1,0:T(8,128)(2,1)S(1)}, u32[]{:S(2)}, u32[]{:S(2)}) async-start(bf16[32,128,128]{2,1,0:T(8,128)(2,1)} %bitcast.16), calls=%async_computation.3 | async-start | bytes 2097152 | tf_op jit(solution)/shard_map/all_to_all | solution.py:394
  92.4 1.7 %collective-permute-start.1 = (bf16[160,128]{1,0:T(8,128)(2,1)S(1)}, bf16[160,128]{1,0:T(8,128)(2,1)S(1)}, u32[]{:S(2)}, u32[]{:S(2)}) collective-permute-start(bf16[160,128]{1,0:T(8,128)(2,1)S(1)} %convert_reduce_fusion), channel_id=1, source_target_pairs={{0,32},{32,0},{64,96},{96,64},{128,160},{160,128},{192,224},{224,1... | collective-permute-start | bytes 122888 | tf_op jit(solution)/shard_map/ppermute | solution.py:327
  94.1 3.0 %collective-permute-start.2 = (bf16[160,128]{1,0:T(8,128)(2,1)S(1)}, bf16[160,128]{1,0:T(8,128)(2,1)S(1)}, u32[]{:S(2)}, u32[]{:S(2)}) collective-permute-start(bf16[160,128]{1,0:T(8,128)(2,1)S(1)} %convert_reduce_fusion), channel_id=1, source_target_pairs={{0,64},{32,96},{64,0},{96,32},{128,192},{160,224},{192,128},{224,1... | collective-permute-start | bytes 122888 | tf_op jit(solution)/shard_map/ppermute | solution.py:327
  97.1 2.2 %collective-permute-done.2 = bf16[160,128]{1,0:T(8,128)(2,1)S(1)} collective-permute-done((bf16[160,128]{1,0:T(8,128)(2,1)S(1)}, bf16[160,128]{1,0:T(8,128)(2,1)S(1)}, u32[]{:S(2)}, u32[]{:S(2)}) %collective-permute-start.2) | collective-permute-done | bytes 40992 | tf_op jit(solution)/shard_map/ppermute | solution.py:327
  99.3 2.8 %collective-permute-done.3 = bf16[160,128]{1,0:T(8,128)(2,1)S(1)} collective-permute-done((bf16[160,128]{1,0:T(8,128)(2,1)S(1)}, bf16[160,128]{1,0:T(8,128)(2,1)S(1)}, u32[]{:S(2)}, u32[]{:S(2)}) %collective-permute-start.3) | collective-permute-done | bytes 40992 | tf_op jit(solution)/shard_map/ppermute | solution.py:327
  102.1 4.3 %collective-permute-start.4 = (bf16[160,128]{1,0:T(8,128)(2,1)S(1)}, bf16[160,128]{1,0:T(8,128)(2,1)S(1)}, u32[]{:S(2)}, u32[]{:S(2)}) collective-permute-start(bf16[160,128]{1,0:T(8,128)(2,1)S(1)} %add_convert_fusion.1), channel_id=1, source_target_pairs={{0,128},{32,160},{64,192},{96,224},{128,0},{160,32},{192,64},{224,... | collective-permute-start | bytes 122888 | tf_op jit(solution)/shard_map/ppermute | solution.py:327
  106.4 2.8 %collective-permute-done.4 = bf16[160,128]{1,0:T(8,128)(2,1)S(1)} collective-permute-done((bf16[160,128]{1,0:T(8,128)(2,1)S(1)}, bf16[160,128]{1,0:T(8,128)(2,1)S(1)}, u32[]{:S(2)}, u32[]{:S(2)}) %collective-permute-start.4) | collective-permute-done | bytes 40992 | tf_op jit(solution)/shard_map/ppermute | solution.py:327
  109.2 0.4 all-to-all-done.3
  109.8 16.0 %all_to_all.46 = bf16[16,160,128]{2,1,0:T(8,128)(2,1)S(1)} all-to-all(bf16[16,160,128]{2,1,0:T(8,128)(2,1)S(1)} %broadcast_in_dim.14), channel_id=1, replica_groups={{0,2,4,6,8,10,12,14,16,18,20,22,24,26,28,30},{1,3,5,7,9,11,13,15,17,19,..., dimensions={0} | all-to-all | bytes 1310720 | tf_op jit(solution)/shard_map/all_to_all | solution.py:458
  125.8 3.8 %collective-permute-start.5 = (bf16[2560,128]{1,0:T(8,128)(2,1)S(1)}, bf16[2560,128]{1,0:T(8,128)(2,1)S(1)}, u32[]{:S(2)}, u32[]{:S(2)}) collective-permute-start(bf16[2560,128]{1,0:T(8,128)(2,1)S(1)} %bitcast.29), channel_id=1, source_target_pairs={{0,1},{1,0},{2,3},{3,2},{4,5},{5,4},{6,7},{7,6},{8,9},{9,8},{10,11... | collective-permute-start | bytes 1966088 | tf_op jit(solution)/shard_map/ppermute | solution.py:459
  129.7 1.7 %join.1 = bf16[320,256]{1,0:T(8,128)(2,1)} custom-call(s32[1]{0:T(128)} %bitcast.2.pos_ref, s32[8]{0:T(128)S(1)} %bitcast.39, s32[64]{0:T(128)S(1)} %bitcast.42, bf16[64,64,128]{2,1,0:T(8,128)(2,1)S(1)} %bitcast.28, bf16[320,128]{1,0:T(8,128)(2,1)S(1)} %get-tuple-element.21.prompt_grad_ref.value_ref), custom_call_target="tpu_custom_call" | custom-call | tf_op jit(solution)/shard_map/join/pallas_call | solution.py:469
  131.4 1.1 finish.1
  (23 shorter events, 0.3 us)
Async XLA Ops:
  1.8 37.0 %copy-start.2 = (bf16[1,128,640]{2,1,0:T(8,128)(2,1)S(1)}, bf16[1,128,640]{2,1,0:T(8,128)(2,1)}, u32[]{:S(2)}) copy-start(bf16[1,128,640]{2,1,0:T(8,128)(2,1)} %param.9) | copy-start | bytes 491524
  1.9 37.0 %copy-start.3 = (bf16[1,128,256]{2,1,0:T(8,128)(2,1)S(1)}, bf16[1,128,256]{2,1,0:T(8,128)(2,1)}, u32[]{:S(2)}) copy-start(bf16[1,128,256]{2,1,0:T(8,128)(2,1)} %param.10) | copy-start | bytes 196612
  1.9 37.0 %copy-start.4 = (bf16[1,128,640]{2,1,0:T(8,128)(2,1)S(1)}, bf16[1,128,640]{2,1,0:T(8,128)(2,1)}, u32[]{:S(2)}) copy-start(bf16[1,128,640]{2,1,0:T(8,128)(2,1)} %param.11) | copy-start | bytes 491524
  1.9 37.0 %copy-start.5 = (s32[1,8]{1,0:T(1,128)S(1)}, s32[1,8]{1,0:T(1,128)}, u32[]{:S(2)}) copy-start(s32[1,8]{1,0:T(1,128)} %blocks_hbm.1) | copy-start | bytes 100
  1.9 37.0 %copy-start.6 = (s32[1,64]{1,0:T(1,128)S(1)}, s32[1,64]{1,0:T(1,128)}, u32[]{:S(2)}) copy-start(s32[1,64]{1,0:T(1,128)} %order_hbm.1) | copy-start | bytes 772
  1.9 37.0 %copy-start.7 = (s32[1,2]{1,0:T(1,128)S(1)}, s32[1,2]{1,0:T(1,128)}, u32[]{:S(2)}) copy-start(s32[1,2]{1,0:T(1,128)} %param.17) | copy-start | bytes 28
  38.9 27.2 %copy-start = (bf16[1,5,64,5120]{3,2,1,0:T(8,128)(2,1)S(1)}, bf16[1,5,64,5120]{3,2,1,0:T(8,128)(2,1)}, u32[]{:S(2)}) copy-start(bf16[1,5,64,5120]{3,2,1,0:T(8,128)(2,1)} %param.14) | copy-start | bytes 9830404
  45.2 20.8 %copy-start.1 = (bf16[1,128,5120]{2,1,0:T(8,128)(2,1)S(1)}, bf16[1,128,5120]{2,1,0:T(8,128)(2,1)}, u32[]{:S(2)}) copy-start(bf16[1,128,5120]{2,1,0:T(8,128)(2,1)} %param.13) | copy-start | bytes 3932164
  68.0 2.2 %collective-permute-start = (bf16[2560,128]{1,0:T(8,128)(2,1)S(1)}, bf16[2560,128]{1,0:T(8,128)(2,1)S(1)}, u32[]{:S(2)}, u32[]{:S(2)}) collective-permute-start(bf16[2560,128]{1,0:T(8,128)(2,1)S(1)} %get-tuple-element.22), channel_id=1, source_target_pairs={{0,1},{1,0},{2,3},{3,2},{4,5},{5,4},{6,7},{7,6},{8,9},{9,8},{10,11... | collective-permute-start | bytes 1966088 | tf_op jit(solution)/shard_map/ppermute | solution.py:437
  71.2 16.0 %all-to-all-start.2 = ((bf16[16,160,128]{2,1,0:T(8,128)(2,1)}), bf16[16,160,128]{2,1,0:T(8,128)(2,1)S(1)}, u32[]{:S(2)}, u32[]{:S(2)}) async-start(bf16[16,160,128]{2,1,0:T(8,128)(2,1)} %bitcast.44), calls=%async_computation.2 | async-start | bytes 1310720 | tf_op jit(solution)/shard_map/all_to_all | solution.py:450
  87.3 22.4 %all-to-all-start.3 = ((bf16[32,128,128]{2,1,0:T(8,128)(2,1)}), bf16[32,128,128]{2,1,0:T(8,128)(2,1)S(1)}, u32[]{:S(2)}, u32[]{:S(2)}) async-start(bf16[32,128,128]{2,1,0:T(8,128)(2,1)} %bitcast.16), calls=%async_computation.3 | async-start | bytes 2097152 | tf_op jit(solution)/shard_map/all_to_all | solution.py:394
  92.4 4.7 %collective-permute-start.1 = (bf16[160,128]{1,0:T(8,128)(2,1)S(1)}, bf16[160,128]{1,0:T(8,128)(2,1)S(1)}, u32[]{:S(2)}, u32[]{:S(2)}) collective-permute-start(bf16[160,128]{1,0:T(8,128)(2,1)S(1)} %convert_reduce_fusion), channel_id=1, source_target_pairs={{0,32},{32,0},{64,96},{96,64},{128,160},{160,128},{192,224},{224,1... | collective-permute-start | bytes 122888 | tf_op jit(solution)/shard_map/ppermute | solution.py:327
  94.1 5.2 %collective-permute-start.2 = (bf16[160,128]{1,0:T(8,128)(2,1)S(1)}, bf16[160,128]{1,0:T(8,128)(2,1)S(1)}, u32[]{:S(2)}, u32[]{:S(2)}) collective-permute-start(bf16[160,128]{1,0:T(8,128)(2,1)S(1)} %convert_reduce_fusion), channel_id=1, source_target_pairs={{0,64},{32,96},{64,0},{96,32},{128,192},{160,224},{192,128},{224,1... | collective-permute-start | bytes 122888 | tf_op jit(solution)/shard_map/ppermute | solution.py:327
  97.1 4.9 %collective-permute-start.3 = (bf16[160,128]{1,0:T(8,128)(2,1)S(1)}, bf16[160,128]{1,0:T(8,128)(2,1)S(1)}, u32[]{:S(2)}, u32[]{:S(2)}) collective-permute-start(bf16[160,128]{1,0:T(8,128)(2,1)S(1)} %convert_reduce_fusion), channel_id=1, source_target_pairs={{0,96},{32,64},{64,32},{96,0},{128,224},{160,192},{192,160},{224,1... | collective-permute-start | bytes 122888 | tf_op jit(solution)/shard_map/ppermute | solution.py:327
  102.1 7.1 %collective-permute-start.4 = (bf16[160,128]{1,0:T(8,128)(2,1)S(1)}, bf16[160,128]{1,0:T(8,128)(2,1)S(1)}, u32[]{:S(2)}, u32[]{:S(2)}) collective-permute-start(bf16[160,128]{1,0:T(8,128)(2,1)S(1)} %add_convert_fusion.1), channel_id=1, source_target_pairs={{0,128},{32,160},{64,192},{96,224},{128,0},{160,32},{192,64},{224,... | collective-permute-start | bytes 122888 | tf_op jit(solution)/shard_map/ppermute | solution.py:327
  125.8 5.6 %collective-permute-start.5 = (bf16[2560,128]{1,0:T(8,128)(2,1)S(1)}, bf16[2560,128]{1,0:T(8,128)(2,1)S(1)}, u32[]{:S(2)}, u32[]{:S(2)}) collective-permute-start(bf16[2560,128]{1,0:T(8,128)(2,1)S(1)} %bitcast.29), channel_id=1, source_target_pairs={{0,1},{1,0},{2,3},{3,2},{4,5},{5,4},{6,7},{7,6},{8,9},{9,8},{10,11... | collective-permute-start | bytes 1966088 | tf_op jit(solution)/shard_map/ppermute | solution.py:459

commit v4 on v3

--- a/solution.py
+++ b/solution.py
@@ -18,7 +18,6 @@
 LOG2E = 1.4426950408889634
 OWN_BLOCKS = 4
 CHUNK = 640
-NN = (((1,), (0,)), ((), ()))
 NT = (((1,), (1,)), ((), ()))
 TN = (((0,), (0,)), ((), ()))
 
@@ -76,10 +75,6 @@
     lax.fori_loop(0, out_ref.shape[0], body, 0, unroll=8)
 
 
-def stacked_heads(ref, rows):
-    return jnp.concatenate([ref[rows, h * HD : (h + 1) * HD] for h in range(HEADS)], axis=0)
-
-
 def attention_kernel(
     owners,
     pos_ref,
@@ -90,41 +85,46 @@
     own_ref,
     grad_ref,
     got_ref,
+    dq_ref,
+    down_ref,
     down_v_ref,
+    back_k_hbm,
     back_v_ref,
-    sgrad_hbm,
     score_ref,
     pgrad_ref,
-    sgrad_ref,
+    back_k_ref,
     sems,
 ):
     f32, bf16 = jnp.float32, jnp.bfloat16
     chunk = OWN_BLOCKS * PB
     chunks = owners // OWN_BLOCKS
     factor = SCALING * LOG2E
+    copies = []
     for member in range(RESP_DEV):
         prompt = order_ref[pos_ref[0] * RESP_DEV + member] >> 3
         begin = first_block(blocks_ref, prompt)
         count = blocks_ref[prompt]
         rows = slice(member * RLEN, (member + 1) * RLEN)
-        q = stacked_heads(query_ref, rows)
-        g = stacked_heads(grad_ref, rows)
+        q = jnp.concatenate(
+            [query_ref[rows, h * HD : (h + 1) * HD] for h in range(HEADS)], axis=0
+        )
+        g = jnp.concatenate([grad_ref[rows, h * HD : (h + 1) * HD] for h in range(HEADS)], axis=0)
         row_ids = lax.broadcasted_iota(jnp.int32, (ROWS, HD), 0) & (RLEN - 1)
         g = jnp.where(row_ids < len_ref[member], g, jnp.zeros_like(g))
 
-        def part_of(i):
-            return slice(i * OWN_BLOCKS, (i + 1) * OWN_BLOCKS)
+        def keys_of(i):
+            if i < chunks:
+                part = got_ref[i * OWN_BLOCKS : (i + 1) * OWN_BLOCKS, member]
+                return part.reshape(chunk, 2 * HD)
+            return own_ref[rows, :]
 
         def rows_of(i):
             return slice(i * chunk, i * chunk + (chunk if i < chunks else RLEN))
 
         top = jnp.full((8, ROWS), -1e30, f32)
         for i in range(chunks + 1):
-            if i < chunks:
-                k = got_ref[part_of(i), member, :, :HD].reshape(chunk, HD)
-            else:
-                k = own_ref[rows, :HD]
-            s = lax.dot_general(k, q, NT, preferred_element_type=f32)
+            kv = keys_of(i)
+            s = lax.dot_general(kv[:, :HD], q, NT, preferred_element_type=f32)
             if i < chunks:
                 seen = []
                 for j in range(OWN_BLOCKS):
@@ -142,11 +142,8 @@
         total = jnp.zeros((8, ROWS), f32)
         mixed = jnp.zeros((8, ROWS), f32)
         for i in range(chunks + 1):
-            if i < chunks:
-                v = got_ref[part_of(i), member, :, HD:].reshape(chunk, HD)
-            else:
-                v = own_ref[rows, HD:]
-            pg = lax.dot_general(v, g, NT, preferred_element_type=f32)
+            kv = keys_of(i)
+            pg = lax.dot_general(kv[:, HD:], g, NT, preferred_element_type=f32)
             e = jnp.exp2((score_ref[rows_of(i), :] - top) * factor)
             score_ref[rows_of(i), :] = e
             pgrad_ref[rows_of(i), :] = pg
@@ -154,69 +151,39 @@
             mixed = mixed + jnp.sum((e * pg).reshape(-1, 8, ROWS), axis=0)
         inverse = 1.0 / jnp.sum(total, axis=0, keepdims=True)
         row_total = jnp.sum(mixed, axis=0, keepdims=True) * inverse
-        for i in range(chunks + 1):
-            p = score_ref[rows_of(i), :] * inverse
-            sgrad_ref[member, rows_of(i), :] = (
-                p * (pgrad_ref[rows_of(i), :] - row_total)
-            ).astype(bf16)
-            dv = lax.dot_general(p.astype(bf16), g, NN, preferred_element_type=f32).astype(bf16)
-            if i < chunks:
-                back_v_ref[part_of(i), member] = dv.reshape(OWN_BLOCKS, PB, HD)
-            else:
-                down_v_ref[rows, :] = dv
-        pltpu.make_async_copy(sgrad_ref.at[member], sgrad_hbm.at[member], sems.at[member]).start()
-    for member in range(RESP_DEV):
-        pltpu.make_async_copy(sgrad_ref.at[member], sgrad_hbm.at[member], sems.at[member]).wait()
-
-
-def query_key_kernel(
-    owners,
-    query_ref,
-    own_ref,
-    got_ref,
-    sgrad_hbm,
-    down_v_ref,
-    dq_ref,
-    down_ref,
-    back_k_ref,
-    sgrad_ref,
-    sems,
-):
-    copies = [
-        pltpu.make_async_copy(sgrad_hbm.at[member], sgrad_ref.at[member], sems.at[member])
-        for member in range(RESP_DEV)
-    ]
-    for copy in copies:
-        copy.start()
-    f32, bf16 = jnp.float32, jnp.bfloat16
-    chunk = OWN_BLOCKS * PB
-    chunks = owners // OWN_BLOCKS
-    for member in range(RESP_DEV):
-        rows = slice(member * RLEN, (member + 1) * RLEN)
-        q = stacked_heads(query_ref, rows)
-        copies[member].wait()
         dqt = jnp.zeros((HD, ROWS), f32)
         for i in range(chunks + 1):
-            part = slice(i * OWN_BLOCKS, (i + 1) * OWN_BLOCKS)
-            ds = sgrad_ref[member, i * chunk : i * chunk + (chunk if i < chunks else RLEN), :]
-            dk = lax.dot_general(ds, q, NN, preferred_element_type=f32) * SCALING
+            kv = keys_of(i)
+            p = score_ref[rows_of(i), :] * inverse
+            ds = (p * (pgrad_ref[rows_of(i), :] - row_total)).astype(bf16)
+            dk = lax.dot_general(ds, q, (((1,), (0,)), ((), ())), preferred_element_type=f32)
+            dv = lax.dot_general(
+                p.astype(bf16), g, (((1,), (0,)), ((), ())), preferred_element_type=f32
+            )
+            dk, dv = (dk * SCALING).astype(bf16), dv.astype(bf16)
             if i < chunks:
-                k = got_ref[part, member, :, :HD].reshape(chunk, HD)
-                back_k_ref[part, member] = dk.astype(bf16).reshape(OWN_BLOCKS, PB, HD)
+                part = slice(i * OWN_BLOCKS, (i + 1) * OWN_BLOCKS)
+                back_k_ref[member, part] = dk.reshape(OWN_BLOCKS, PB, HD)
+                back_v_ref[part, member] = dv.reshape(OWN_BLOCKS, PB, HD)
             else:
-                k = own_ref[rows, :HD]
-                down_ref[rows, :HD] = dk.astype(bf16)
-            dqt = dqt + lax.dot_general(k, ds, TN, preferred_element_type=f32)
+                down_ref[rows, :HD] = dk
+                down_ref[rows, HD:] = dv
+                down_v_ref[rows, :] = dv
+            dqt = dqt + lax.dot_general(kv[:, :HD], ds, TN, preferred_element_type=f32)
+        copies.append(
+            pltpu.make_async_copy(back_k_ref.at[member], back_k_hbm.at[:, member], sems.at[member])
+        )
+        copies[-1].start()
         dq = (dqt * SCALING).T.astype(bf16)
         for h in range(HEADS):
             dq_ref[rows, h * HD : (h + 1) * HD] = dq[h * RLEN : (h + 1) * RLEN]
-    down_ref[:, HD:] = down_v_ref[...]
-
-
-def half_weights(core, resp_in_ref, resp_grad, prompt_in_ref, prompt_grad, weight_ref):
-    half = weight_ref.shape[0]
-    for i in range(half // CHUNK):
-        place = pl.ds(pl.multiple_of(core * half + i * CHUNK, HD), CHUNK)
+    for copy in copies:
+        copy.wait()
+
+
+def some_weights(start, resp_in_ref, resp_grad, prompt_in_ref, prompt_grad, weight_ref):
+    for i in range(weight_ref.shape[0] // CHUNK):
+        place = pl.ds(pl.multiple_of(start + i * CHUNK, HD), CHUNK)
         term = lax.dot_general(
             resp_in_ref[:, place], resp_grad, TN, preferred_element_type=jnp.float32
         )
@@ -257,7 +224,8 @@
     prompt_grad = acc_ref[...].reshape(out_ref.shape).astype(jnp.bfloat16)
     out_ref[...] = prompt_grad
     other = 1 - (pos_ref[0] & 1)
-    half_weights(other, resp_in_ref, resp_grad_ref[...], prompt_in_ref, prompt_grad, weight_ref)
+    start = other * (resp_in_ref.shape[1] // 2)
+    some_weights(start, resp_in_ref, resp_grad_ref[...], prompt_in_ref, prompt_grad, weight_ref)
 
 
 def join_kernel(
@@ -269,10 +237,10 @@
 
 
 def weight_kernel(
-    pos_ref, resp_in_ref, resp_grad_ref, prompt_in_ref, prompt_grad_ref, weight_ref
-):
-    half_weights(
-        pos_ref[0] & 1,
+    flip, offset, pos_ref, resp_in_ref, resp_grad_ref, prompt_in_ref, prompt_grad_ref, weight_ref
+):
+    some_weights(
+        ((pos_ref[0] & 1) ^ flip) * (resp_in_ref.shape[1] // 2) + offset,
         resp_in_ref,
         resp_grad_ref[...],
         prompt_in_ref,
@@ -353,7 +321,7 @@
     packed = pl.pallas_call(
         functools.partial(pack_kernel, owners),
         out_shape=jax.ShapeDtypeStruct((responses, PB, 2 * HD), bf16),
-        in_specs=[smem()] + [hbm()] * 3,
+        in_specs=[smem()] + [pl.BlockSpec(memory_space=pltpu.HBM)] * 3,
         out_specs=vmem(),
         scratch_shapes=[
             pltpu.SMEM(blocks.shape, jnp.int32),
@@ -371,46 +339,31 @@
 
     keys = owners * PB + RLEN
     part_shape = jax.ShapeDtypeStruct((owners, RESP_DEV, PB, HD), bf16)
-    down_v, part_v, score_grad = pl.pallas_call(
+    d_queries, d_resp_kv, d_value_own, part_k, part_v = pl.pallas_call(
         functools.partial(attention_kernel, owners),
         out_shape=(
+            jax.ShapeDtypeStruct((RESP_DEV * RLEN, HEADS * HD), bf16),
+            jax.ShapeDtypeStruct((RESP_DEV * RLEN, 2 * HD), bf16),
             jax.ShapeDtypeStruct((RESP_DEV * RLEN, HD), bf16),
+            pltpu.HBM(part_shape.shape, bf16),
             part_shape,
-            pltpu.HBM((RESP_DEV, keys, ROWS), bf16),
         ),
         in_specs=[smem()] * 4 + [vmem()] * 4,
-        out_specs=[vmem(), vmem(), hbm()],
+        out_specs=[vmem(), vmem(), vmem(), hbm(), vmem()],
         scratch_shapes=[
             pltpu.VMEM((keys, ROWS), f32),
             pltpu.VMEM((keys, ROWS), f32),
-            pltpu.VMEM((RESP_DEV, keys, ROWS), bf16),
+            pltpu.VMEM((RESP_DEV, owners, PB, HD), bf16),
             pltpu.SemaphoreType.DMA((RESP_DEV,)),
         ],
         compiler_params=params(),
         name="attention",
     )(pos, blocks, order, lengths, queries[0], resp_kv[0], grad_out[0], fetched)
-
     def to_owners(part):
         got = lax.all_to_all(part.reshape(responses * PB, HD), "seq", 0, 0, tiled=True)
         return got.reshape(responses, PB, HD)
 
     returned_v = to_owners(part_v)
-    d_queries, d_resp_kv, part_k = pl.pallas_call(
-        functools.partial(query_key_kernel, owners),
-        out_shape=(
-            jax.ShapeDtypeStruct((RESP_DEV * RLEN, HEADS * HD), bf16),
-            jax.ShapeDtypeStruct((RESP_DEV * RLEN, 2 * HD), bf16),
-            part_shape,
-        ),
-        in_specs=[vmem(), vmem(), vmem(), hbm(), vmem()],
-        out_specs=[vmem()] * 3,
-        scratch_shapes=[
-            pltpu.VMEM((RESP_DEV, keys, ROWS), bf16),
-            pltpu.SemaphoreType.DMA((RESP_DEV,)),
-        ],
-        compiler_params=params(),
-        name="query_key",
-    )(queries[0], resp_kv[0], fetched, in_hbm(score_grad), down_v)
 
     rows, prompt_rows = RESP_DEV * RLEN, slot_rows * PB
     width = resp_inputs.shape[2]
@@ -422,7 +375,7 @@
         functools.partial(combine_kernel, owners),
         out_shape=(
             jax.ShapeDtypeStruct((prompt_rows, HD), bf16),
-            jax.ShapeDtypeStruct((half, HD), bf16),
+            jax.ShapeDtypeStruct((half // 2, HD), bf16),
         ),
         in_specs=[smem()] * 3 + [vmem()] * 4,
         out_specs=[vmem()] * 2,
@@ -432,19 +385,24 @@
         ],
         compiler_params=params(),
         name="combine",
-    )(pos, blocks, order, returned_v, resp_in, down_v, prompt_in)
+    )(pos, blocks, order, returned_v, resp_in, d_value_own, prompt_in)
     swap = [(i, i ^ 1) for i in range(owners)]
-    from_twin = lax.ppermute(sent, "seq", swap)
-    kept = pl.pallas_call(
-        weight_kernel,
-        out_shape=jax.ShapeDtypeStruct((half, HD), bf16),
-        in_specs=[smem()] + [vmem()] * 4,
-        out_specs=vmem(),
-        compiler_params=params(),
-        name="weights",
-    )(pos, resp_in, down_v, prompt_in, d_value)
-
-    both = (kept.astype(f32) + from_twin.astype(f32)).astype(bf16)
+
+    def weights(flip, offset, count):
+        return pl.pallas_call(
+            functools.partial(weight_kernel, flip, offset),
+            out_shape=jax.ShapeDtypeStruct((count, HD), bf16),
+            in_specs=[smem()] + [vmem()] * 4,
+            out_specs=vmem(),
+            compiler_params=params(),
+            name="weights",
+        )(pos, resp_in, d_value_own, prompt_in, d_value)
+
+    more = weights(1, half // 2, half // 2)
+    swap = [(i, i ^ 1) for i in range(owners)]
+    from_twin = [lax.ppermute(x, "seq", swap) for x in (sent, more)]
+    kept = weights(0, 0, half)
+    both = (kept.astype(f32) + jnp.concatenate(from_twin, axis=0).astype(f32)).astype(bf16)
     twins = [list(range(c, owners, 2)) for c in range(2)]
     chips = owners // 2
     shares = lax.all_to_all(both, "seq", 0, 0, tiled=True, axis_index_groups=twins)

time: 133 us -> 133 us (level)
  blocking collectives: 73.8 us -> 89.3 us
  waiting for transfers between devices: 17.1 us -> 8.97 us
  starting transfers between devices: 22 us -> 18.4 us
  Pallas kernels: 17.4 us -> 14.6 us
    all_to_all x0 -> x1, blocking collectives: none -> 15.7 us  [local(): lax.all_to_all(both, 'seq', 0, 0, tiled=True, axis_index_groups=twins)]
    all_to_all x1 -> x0, waiting for transfers between devices: 8.02 us -> none  [local(): lax.all_to_all(both, 'seq', 0, 0, tiled=True, axis_index_groups=twins)]
    pallas_call x2, Pallas kernels: 5.26 us -> 1.48 us  [weights(): pl.pallas_call(functools.partial(weight_kernel, flip, offset), out_shape=...]
    all_to_all x1 -> x0, starting transfers between devices: 3.59 us -> none  [local(): lax.all_to_all(both, 'seq', 0, 0, tiled=True, axis_index_groups=twins)]
    pallas_call x1, Pallas kernels: 6.29 us -> 7.65 us  [local(): pl.pallas_call(functools.partial(attention_kernel, owners), out_shape=(ja...]
  transfers between devices with their start and end apart: 8 -> 8, of which waited for: 7 -> 8; matrix products, arithmetic and copies ran while one was open for 0% -> 0% of each run, Pallas kernels for 5% -> 2%
where the time goes in v4:
time: 133 us
  blocking collectives  89.3 us (67%)
  starting transfers between devices  18.4 us (14%)
  Pallas kernels  14.6 us (11%)
  waiting for transfers between devices  8.97 us (7%)
    all_to_all x1, blocking collectives, local(): lax.all_to_all(packed.reshape(responses * PB, 2 * HD), 'seq', 0, 0, tiled...  36.9 us
    all_to_all x1, blocking collectives, to_owners(): lax.all_to_all(part.reshape(responses * PB, HD), 'seq', 0, 0, tiled=True)  20.8 us
    all_to_all x1, blocking collectives, local(): lax.all_to_all(copies, 'seq', 0, 0, tiled=True, axis_index_groups=twins)  15.9 us
    all_to_all x1, blocking collectives, local(): lax.all_to_all(both, 'seq', 0, 0, tiled=True, axis_index_groups=twins)  15.7 us
    ppermute x4, starting transfers between devices, grp_sum(): terms.append(lax.ppermute(own, 'grp', pairs).astype(jnp.float32))  9.01 us
    ppermute x4, waiting for transfers between devices, grp_sum(): terms.append(lax.ppermute(own, 'grp', pairs).astype(jnp.float32))  7.78 us
    pallas_call x1, Pallas kernels, local(): pl.pallas_call(functools.partial(attention_kernel, owners), out_shape=(ja...  7.65 us
    all_to_all x1, starting transfers between devices, to_owners(): lax.all_to_all(part.reshape(responses * PB, HD), 'seq', 0, 0, tiled=True)  4.87 us
  transfers between devices with their start and end apart: 8, of which 8 were waited for; matrix products, arithmetic and copies ran while one was open for 0% of the time, Pallas kernels for 2%

profile of v4, /device:TPU:1, one launch (start us, length us, event | category | flops | bytes accessed | tf_op | source)
XLA Modules:
  0.0 132.6 jit_solution(12413546753232612208)
XLA Ops:
  0.6 1.2 pack.1
  1.9 36.9 %all_to_all.44 = bf16[32,128,256]{2,1,0:T(8,128)(2,1)S(1)} all-to-all(bf16[32,128,256]{2,1,0:T(8,128)(2,1)S(1)} %bitcast.27), channel_id=1, replica_groups=mesh['grp'=8,'seq'=32] {'seq'}, dimensions={0} | all-to-all | bytes 4194304 | tf_op jit(solution)/shard_map/all_to_all | solution.py:336
  38.9 7.6 %attention.1 = (bf16[128,640]{1,0:T(8,128)(2,1)}, bf16[128,256]{1,0:T(8,128)(2,1)}, bf16[128,128]{1,0:T(8,128)(2,1)S(1)}, bf16[32,2,64,128]{3,2,1,0:T(8,128)(2,1)}, bf16[32,2,64,128]{3,2,1,0:T(8,128)(2,1)S(1)}) custom-call(s32[1]{0:T(128)} %bitcast.pos_ref, s32[8]{0:T(128)S(1)} %bitcast.36, s32[64]{0:T(128)S(1)} %bitcast.39, s32[2]{0:T(128)S(1)} %bitcast.42, ...), custom_call_target="tpu_custom_call" | custom-call | tf_op jit(solution)/shard_map/attention/pallas_call | solution.py:342
  46.6 20.8 %all_to_all.45 = bf16[32,128,128]{2,1,0:T(8,128)(2,1)S(1)} all-to-all(bf16[32,128,128]{2,1,0:T(8,128)(2,1)S(1)} %bitcast.32), channel_id=1, replica_groups=mesh['grp'=8,'seq'=32] {'seq'}, dimensions={0} | all-to-all | bytes 2097152 | tf_op jit(solution)/shard_map/all_to_all | solution.py:363
  67.4 1.6 %combine.1 = (bf16[320,128]{1,0:T(8,128)(2,1)S(1)}, bf16[1280,128]{1,0:T(8,128)(2,1)S(1)}) custom-call(s32[1]{0:T(128)} %bitcast.pos_ref, s32[8]{0:T(128)S(1)} %bitcast.37, s32[64]{0:T(128)S(1)} %bitcast.40, bf16[64,64,128]{2,1,0:T(8,128)(2,1)S(1)} %bitcast.28, bf16[128,5120]{1,0:T(8,128)(2,1)S(1)} %bitcast.23, ...), custom_call_target="tpu_custom_call" | custom-call | tf_op jit(solution)/shard_map/combine/pallas_call | solution.py:374
  69.0 0.6 weights.3
  69.5 0.5 collective-permute-start.1
  70.1 0.9 weights.2
  71.1 0.2 collective-permute-done.1
  71.3 0.5 collective-permute-done
  71.8 0.2 add_convert_fusion
  71.9 15.7 %all_to_all.46 = bf16[16,160,128]{2,1,0:T(8,128)(2,1)S(1)} all-to-all(bf16[16,160,128]{2,1,0:T(8,128)(2,1)S(1)} %bitcast.43), channel_id=1, replica_groups={{0,2,4,6,8,10,12,14,16,18,20,22,24,26,28,30},{1,3,5,7,9,11,13,15,17,19,..., dimensions={0} | all-to-all | bytes 1310720 | tf_op jit(solution)/shard_map/all_to_all | solution.py:408
  87.7 4.9 %all-to-all-start.3 = ((bf16[32,128,128]{2,1,0:T(8,128)(2,1)}), bf16[32,128,128]{2,1,0:T(8,128)(2,1)S(1)}, u32[]{:S(2)}, u32[]{:S(2)}) async-start(bf16[32,128,128]{2,1,0:T(8,128)(2,1)} %bitcast.16), calls=%async_computation.3 | async-start | bytes 2097152 | tf_op jit(solution)/shard_map/all_to_all | solution.py:363
  92.6 3.1 %collective-permute-start.3 = (bf16[160,128]{1,0:T(8,128)(2,1)S(1)}, bf16[160,128]{1,0:T(8,128)(2,1)S(1)}, u32[]{:S(2)}, u32[]{:S(2)}) collective-permute-start(bf16[160,128]{1,0:T(8,128)(2,1)S(1)} %convert_reduce_fusion), channel_id=1, source_target_pairs={{0,64},{32,96},{64,0},{96,32},{128,192},{160,224},{192,128},{224,1... | collective-permute-start | bytes 122888 | tf_op jit(solution)/shard_map/ppermute | solution.py:295
  95.7 1.6 %collective-permute-start.2 = (bf16[160,128]{1,0:T(8,128)(2,1)S(1)}, bf16[160,128]{1,0:T(8,128)(2,1)S(1)}, u32[]{:S(2)}, u32[]{:S(2)}) collective-permute-start(bf16[160,128]{1,0:T(8,128)(2,1)S(1)} %convert_reduce_fusion), channel_id=1, source_target_pairs={{0,32},{32,0},{64,96},{96,64},{128,160},{160,128},{192,224},{224,1... | collective-permute-start | bytes 122888 | tf_op jit(solution)/shard_map/ppermute | solution.py:295
  97.3 1.6 %collective-permute-done.2 = bf16[160,128]{1,0:T(8,128)(2,1)S(1)} collective-permute-done((bf16[160,128]{1,0:T(8,128)(2,1)S(1)}, bf16[160,128]{1,0:T(8,128)(2,1)S(1)}, u32[]{:S(2)}, u32[]{:S(2)}) %collective-permute-start.2) | collective-permute-done | bytes 40992 | tf_op jit(solution)/shard_map/ppermute | solution.py:295
  99.0 3.3 %collective-permute-done.4 = bf16[160,128]{1,0:T(8,128)(2,1)S(1)} collective-permute-done((bf16[160,128]{1,0:T(8,128)(2,1)S(1)}, bf16[160,128]{1,0:T(8,128)(2,1)S(1)}, u32[]{:S(2)}, u32[]{:S(2)}) %collective-permute-start.4) | collective-permute-done | bytes 40992 | tf_op jit(solution)/shard_map/ppermute | solution.py:295
  102.3 4.3 %collective-permute-start.5 = (bf16[160,128]{1,0:T(8,128)(2,1)S(1)}, bf16[160,128]{1,0:T(8,128)(2,1)S(1)}, u32[]{:S(2)}, u32[]{:S(2)}) collective-permute-start(bf16[160,128]{1,0:T(8,128)(2,1)S(1)} %add_convert_fusion.1), channel_id=1, source_target_pairs={{0,128},{32,160},{64,192},{96,224},{128,0},{160,32},{192,64},{224,... | collective-permute-start | bytes 122888 | tf_op jit(solution)/shard_map/ppermute | solution.py:295
  106.6 2.8 %collective-permute-done.5 = bf16[160,128]{1,0:T(8,128)(2,1)S(1)} collective-permute-done((bf16[160,128]{1,0:T(8,128)(2,1)S(1)}, bf16[160,128]{1,0:T(8,128)(2,1)S(1)}, u32[]{:S(2)}, u32[]{:S(2)}) %collective-permute-start.5) | collective-permute-done | bytes 40992 | tf_op jit(solution)/shard_map/ppermute | solution.py:295
  109.4 0.4 all-to-all-done.3
  109.9 15.9 %all_to_all.47 = bf16[16,160,128]{2,1,0:T(8,128)(2,1)S(1)} all-to-all(bf16[16,160,128]{2,1,0:T(8,128)(2,1)S(1)} %broadcast_in_dim.14), channel_id=1, replica_groups={{0,2,4,6,8,10,12,14,16,18,20,22,24,26,28,30},{1,3,5,7,9,11,13,15,17,19,..., dimensions={0} | all-to-all | bytes 1310720 | tf_op jit(solution)/shard_map/all_to_all | solution.py:416
  125.9 4.0 %collective-permute-start.6 = (bf16[2560,128]{1,0:T(8,128)(2,1)S(1)}, bf16[2560,128]{1,0:T(8,128)(2,1)S(1)}, u32[]{:S(2)}, u32[]{:S(2)}) collective-permute-start(bf16[2560,128]{1,0:T(8,128)(2,1)S(1)} %bitcast.30), channel_id=1, source_target_pairs={{0,1},{1,0},{2,3},{3,2},{4,5},{5,4},{6,7},{7,6},{8,9},{9,8},{10,11... | collective-permute-start | bytes 1966088 | tf_op jit(solution)/shard_map/ppermute | solution.py:417
  129.8 1.7 %join.1 = bf16[320,256]{1,0:T(8,128)(2,1)} custom-call(s32[1]{0:T(128)} %bitcast.pos_ref, s32[8]{0:T(128)S(1)} %bitcast.38, s32[64]{0:T(128)S(1)} %bitcast.41, bf16[64,64,128]{2,1,0:T(8,128)(2,1)S(1)} %bitcast.29, bf16[320,128]{1,0:T(8,128)(2,1)S(1)} %get-tuple-element.19.prompt_grad_ref.value_ref), custom_call_target="tpu_custom_call" | custom-call | tf_op jit(solution)/shard_map/join/pallas_call | solution.py:427
  131.6 1.1 finish.1
  (24 shorter events, 0.5 us)
Async XLA Ops:
  1.8 37.0 %copy-start.2 = (bf16[1,128,640]{2,1,0:T(8,128)(2,1)S(1)}, bf16[1,128,640]{2,1,0:T(8,128)(2,1)}, u32[]{:S(2)}) copy-start(bf16[1,128,640]{2,1,0:T(8,128)(2,1)} %param.9) | copy-start | bytes 491524
  1.9 37.0 %copy-start.3 = (bf16[1,128,640]{2,1,0:T(8,128)(2,1)S(1)}, bf16[1,128,640]{2,1,0:T(8,128)(2,1)}, u32[]{:S(2)}) copy-start(bf16[1,128,640]{2,1,0:T(8,128)(2,1)} %param.11) | copy-start | bytes 491524
  1.9 37.0 %copy-start.4 = (bf16[1,128,256]{2,1,0:T(8,128)(2,1)S(1)}, bf16[1,128,256]{2,1,0:T(8,128)(2,1)}, u32[]{:S(2)}) copy-start(bf16[1,128,256]{2,1,0:T(8,128)(2,1)} %param.10) | copy-start | bytes 196612
  1.9 37.0 %copy-start.5 = (s32[1,8]{1,0:T(1,128)S(1)}, s32[1,8]{1,0:T(1,128)}, u32[]{:S(2)}) copy-start(s32[1,8]{1,0:T(1,128)} %blocks_hbm.1) | copy-start | bytes 100
  1.9 37.0 %copy-start.6 = (s32[1,64]{1,0:T(1,128)S(1)}, s32[1,64]{1,0:T(1,128)}, u32[]{:S(2)}) copy-start(s32[1,64]{1,0:T(1,128)} %order_hbm.1) | copy-start | bytes 772
  1.9 37.0 %copy-start.7 = (s32[1,2]{1,0:T(1,128)S(1)}, s32[1,2]{1,0:T(1,128)}, u32[]{:S(2)}) copy-start(s32[1,2]{1,0:T(1,128)} %param.17) | copy-start | bytes 28
  38.9 28.5 %copy-start = (bf16[1,5,64,5120]{3,2,1,0:T(8,128)(2,1)S(1)}, bf16[1,5,64,5120]{3,2,1,0:T(8,128)(2,1)}, u32[]{:S(2)}) copy-start(bf16[1,5,64,5120]{3,2,1,0:T(8,128)(2,1)} %param.14) | copy-start | bytes 9830404
  46.6 20.8 %copy-start.1 = (bf16[1,128,5120]{2,1,0:T(8,128)(2,1)S(1)}, bf16[1,128,5120]{2,1,0:T(8,128)(2,1)}, u32[]{:S(2)}) copy-start(bf16[1,128,5120]{2,1,0:T(8,128)(2,1)} %param.13) | copy-start | bytes 3932164
  69.5 1.7 %collective-permute-start.1 = (bf16[1280,128]{1,0:T(8,128)(2,1)S(1)}, bf16[1280,128]{1,0:T(8,128)(2,1)S(1)}, u32[]{:S(2)}, u32[]{:S(2)}) collective-permute-start(bf16[1280,128]{1,0:T(8,128)(2,1)S(1)} %weights.3), channel_id=1, source_target_pairs={{0,1},{1,0},{2,3},{3,2},{4,5},{5,4},{6,7},{7,6},{8,9},{9,8},{10,11... | collective-permute-start | bytes 983048 | tf_op jit(solution)/shard_map/ppermute | solution.py:403
  70.0 1.7 %collective-permute-start = (bf16[1280,128]{1,0:T(8,128)(2,1)S(1)}, bf16[1280,128]{1,0:T(8,128)(2,1)S(1)}, u32[]{:S(2)}, u32[]{:S(2)}) collective-permute-start(bf16[1280,128]{1,0:T(8,128)(2,1)S(1)} %get-tuple-element.20), channel_id=1, source_target_pairs={{0,1},{1,0},{2,3},{3,2},{4,5},{5,4},{6,7},{7,6},{8,9},{9,8},{10,11... | collective-permute-start | bytes 983048 | tf_op jit(solution)/shard_map/ppermute | solution.py:403
  87.7 22.2 %all-to-all-start.3 = ((bf16[32,128,128]{2,1,0:T(8,128)(2,1)}), bf16[32,128,128]{2,1,0:T(8,128)(2,1)S(1)}, u32[]{:S(2)}, u32[]{:S(2)}) async-start(bf16[32,128,128]{2,1,0:T(8,128)(2,1)} %bitcast.16), calls=%async_computation.3 | async-start | bytes 2097152 | tf_op jit(solution)/shard_map/all_to_all | solution.py:363
  92.6 4.8 %collective-permute-start.3 = (bf16[160,128]{1,0:T(8,128)(2,1)S(1)}, bf16[160,128]{1,0:T(8,128)(2,1)S(1)}, u32[]{:S(2)}, u32[]{:S(2)}) collective-permute-start(bf16[160,128]{1,0:T(8,128)(2,1)S(1)} %convert_reduce_fusion), channel_id=1, source_target_pairs={{0,64},{32,96},{64,0},{96,32},{128,192},{160,224},{192,128},{224,1... | collective-permute-start | bytes 122888 | tf_op jit(solution)/shard_map/ppermute | solution.py:295
  95.7 3.3 %collective-permute-start.2 = (bf16[160,128]{1,0:T(8,128)(2,1)S(1)}, bf16[160,128]{1,0:T(8,128)(2,1)S(1)}, u32[]{:S(2)}, u32[]{:S(2)}) collective-permute-start(bf16[160,128]{1,0:T(8,128)(2,1)S(1)} %convert_reduce_fusion), channel_id=1, source_target_pairs={{0,32},{32,0},{64,96},{96,64},{128,160},{160,128},{192,224},{224,1... | collective-permute-start | bytes 122888 | tf_op jit(solution)/shard_map/ppermute | solution.py:295
  97.3 4.9 %collective-permute-start.4 = (bf16[160,128]{1,0:T(8,128)(2,1)S(1)}, bf16[160,128]{1,0:T(8,128)(2,1)S(1)}, u32[]{:S(2)}, u32[]{:S(2)}) collective-permute-start(bf16[160,128]{1,0:T(8,128)(2,1)S(1)} %convert_reduce_fusion), channel_id=1, source_target_pairs={{0,96},{32,64},{64,32},{96,0},{128,224},{160,192},{192,160},{224,1... | collective-permute-start | bytes 122888 | tf_op jit(solution)/shard_map/ppermute | solution.py:295
  102.3 7.1 %collective-permute-start.5 = (bf16[160,128]{1,0:T(8,128)(2,1)S(1)}, bf16[160,128]{1,0:T(8,128)(2,1)S(1)}, u32[]{:S(2)}, u32[]{:S(2)}) collective-permute-start(bf16[160,128]{1,0:T(8,128)(2,1)S(1)} %add_convert_fusion.1), channel_id=1, source_target_pairs={{0,128},{32,160},{64,192},{96,224},{128,0},{160,32},{192,64},{224,... | collective-permute-start | bytes 122888 | tf_op jit(solution)/shard_map/ppermute | solution.py:295
  125.9 5.7 %collective-permute-start.6 = (bf16[2560,128]{1,0:T(8,128)(2,1)S(1)}, bf16[2560,128]{1,0:T(8,128)(2,1)S(1)}, u32[]{:S(2)}, u32[]{:S(2)}) collective-permute-start(bf16[2560,128]{1,0:T(8,128)(2,1)S(1)} %bitcast.30), channel_id=1, source_target_pairs={{0,1},{1,0},{2,3},{3,2},{4,5},{5,4},{6,7},{7,6},{8,9},{9,8},{10,11... | collective-permute-start | bytes 1966088 | tf_op jit(solution)/shard_map/ppermute | solution.py:417
